TPU v7x, 32 devices: a whole 2x2x4 slice. The times are simulated.
32 devices in a mesh: dp: 4 (over y, x), expert: 8 (over z, core).
Axes of the slice: x: 2, y: 2, z: 4, core: 2. Of those that a mesh axis runs over, the one named last changes fastest.
Arguments:
- tokens: bfloat16 [8, 1024, 2048], P('expert', 'dp'), may hold values from -6 to 6
- segment_ids: int32 [8, 1024], P('expert'), may hold values from 0 to 2, as said below
- routes: int32 [8, 1024, 8], P('expert', 'dp'), may hold values from 0 to 31, all different within a row; in each aligned block of 256 rows (0 to 255, 256 to 511, ..., all dimensions but the last counted through in order) at most 80 rows name the same one
- w_query: bfloat16 [2048, 4096], P(('dp', 'expert')), may hold values from -0.125 to 0.125
- w_key: bfloat16 [2048, 512], P(('dp', 'expert')), may hold values from -0.125 to 0.125
- w_value: bfloat16 [2048, 512], P(('dp', 'expert')), may hold values from -0.125 to 0.125
- w_output: bfloat16 [4096, 2048], P(('dp', 'expert')), may hold values from -1.5 to 1.5
- w_router: bfloat16 [2048, 32], P(('dp', 'expert')), may hold values from -0.0625 to 0.0625
- gain_attn: bfloat16 [2048], P(('dp', 'expert')), may hold values from 0.5 to 1.5
- gain_moe: bfloat16 [2048], P(('dp', 'expert')), may hold values from 0.5 to 1.5
- gain_query: bfloat16 [128], P(('dp', 'expert')), may hold values from 0.5 to 1.5
- gain_key: bfloat16 [128], P(('dp', 'expert')), may hold values from 0.5 to 1.5
- w_gate: bfloat16 [32, 2048, 768], P('expert'), may hold values from -0.125 to 0.125
- w_up: bfloat16 [32, 2048, 768], P('expert'), may hold values from -0.125 to 0.125
- w_down: bfloat16 [32, 768, 2048], P('expert'), may hold values from -0.875 to 0.875
- cotangent: bfloat16 [8, 1024, 2048], P('expert', 'dp'), may hold values from -6 to 6
Outputs:
- block_out: bfloat16 [8, 1024, 2048], P('expert', 'dp')
- grad_tokens: float32 [8, 1024, 2048], P('expert', 'dp')
- grad_query: float32 [2048, 4096], P(('dp', 'expert'))
- grad_key: float32 [2048, 512], P(('dp', 'expert'))
- grad_value: float32 [2048, 512], P(('dp', 'expert'))
- grad_output: float32 [4096, 2048], P(('dp', 'expert'))
- grad_router: float32 [2048, 32], P(('dp', 'expert'))
- grad_gain_attn: float32 [2048], P(('dp', 'expert'))
- grad_gain_moe: float32 [2048], P(('dp', 'expert'))
- grad_gain_query: float32 [128], P(('dp', 'expert'))
- grad_gain_key: float32 [128], P(('dp', 'expert'))
- grad_gate: float32 [32, 2048, 768], P('expert')
- grad_up: float32 [32, 2048, 768], P('expert')
- grad_down: float32 [32, 768, 2048], P('expert')
Inputs may be any that keep to these rules, and one draw needn't show every extreme that they name: `routes`: each row names 8 different experts; in the 256 rows of one device no expert is named by more than 80 rows, and in some device one expert is named by exactly 80. `segment_ids`: never falling along a sequence; every sequence holds documents 0, 1 and 2: document 0 has 128 or more tokens and ends within the first 256 positions, document 1 ends within the last 256 positions, document 2 has 128 or more tokens.
All inputs are finite; a program needn't handle non-finite values.
Results may differ from a plain program's by a relative error of at most 0.02.
Values may be sent and summed in bfloat16 or wider, within the bound.
A program may use at most 384 MiB of HBM per device.

v0:
```python
import jax
import jax.numpy as jnp
from jax import lax
from jax.experimental import pallas as pl
from jax.experimental.pallas import tpu as pltpu
from jax.sharding import PartitionSpec as P

CAP = 80
Q_BLOCK = 256
HIDDEN_TILE = 256
OWN_ROWS = 8 * CAP
WIDTH_TILE = 512
SIDE = 128
ROW_PARTS = 2
VMEM_BYTES = 60 << 20


EPSILON = 1e-06
ROPE_BASE = 1000000.0
PRECISE = lax.Precision.HIGHEST
F32 = jnp.float32
BF16 = jnp.bfloat16
FREE = pl.CostEstimate(flops=0, bytes_accessed=0, transcendentals=0)


def norm_rows(values, gain_row):
    return (
        values * lax.rsqrt(jnp.mean(values * values, axis=-1, keepdims=True) + EPSILON) * gain_row
    )


def activate(gate_vals, up_vals):
    return gate_vals * jax.nn.sigmoid(gate_vals) * up_vals


def masked_softmax(logits, mask):
    kept = jnp.where(mask, logits, -jnp.inf)
    largest = jnp.max(kept, axis=-1, keepdims=True)
    raised = jnp.where(mask, jnp.exp(logits - largest), 0.0)
    return raised / jnp.sum(raised, axis=-1, keepdims=True)


def nothing(*refs):
    del refs


def after(value, *others):
    anywhere = pl.BlockSpec(memory_space=pl.ANY)
    return pl.pallas_call(
        nothing,
        out_shape=jax.ShapeDtypeStruct(value.shape, value.dtype),
        in_specs=[anywhere] * (1 + len(others)),
        out_specs=anywhere,
        input_output_aliases={0: 0},
    )(value, *others)


def shifted(value, axis, step):
    count = lax.axis_size(axis)
    return lax.ppermute(value, axis, [(i, (i + step) % count) for i in range(count)])


def traded(value, axis, step):
    return lax.ppermute(value, axis, [(i, i ^ step) for i in range(lax.axis_size(axis))])


def gather_blocks(own, axis):
    count, me = lax.axis_size(axis), lax.axis_index(axis)
    whole = jnp.zeros((count, *own.shape), own.dtype)
    whole = lax.dynamic_update_index_in_dim(whole, own, me, 0)
    for step in range(1, count):
        whole = lax.dynamic_update_index_in_dim(whole, traded(own, axis, step), me ^ step, 0)
    return whole


def sum_blocks(blocks, axis):
    count, me = lax.axis_size(axis), lax.axis_index(axis)
    total = lax.dynamic_index_in_dim(blocks, me, 0, keepdims=False).astype(F32)
    for step in range(1, count):
        sent = lax.dynamic_index_in_dim(blocks, me ^ step, 0, keepdims=False)
        total = total + traded(sent, axis, step).astype(F32)
    return total


def sum_peers(blocks):
    count, me = lax.axis_size("expert"), lax.axis_index("expert")
    core, chip, chips = lax.rem(me, 2), lax.div(me, 2), count // 2
    paired = blocks.reshape(chips, 2, *blocks.shape[1:])
    sent = lax.dynamic_index_in_dim(paired, 1 - core, 1, keepdims=False)
    kept = lax.dynamic_index_in_dim(paired, core, 1, keepdims=False)
    got = lax.ppermute(sent, "expert", [(i, i ^ 1) for i in range(count)])
    halves = (kept.astype(F32) + got.astype(F32)).astype(BF16)
    total = lax.dynamic_index_in_dim(halves, chip, 0, keepdims=False).astype(F32)
    for step in range(1, chips):
        sent = lax.dynamic_index_in_dim(halves, lax.rem(chip + step, chips), 0, keepdims=False)
        total = total + shifted(sent, "expert", 2 * step).astype(F32)
    return total


def dot(spec, left, right):
    return jnp.einsum(spec, left, right, preferred_element_type=F32)


def line_sems(chips):
    return [pltpu.SemaphoreType.DMA((chips,))] * 6 + [pltpu.SemaphoreType.DMA]


def send_to(source, target, send_sem, recv_sem, device):
    return pltpu.make_async_remote_copy(
        src_ref=source,
        dst_ref=target,
        send_sem=send_sem,
        recv_sem=recv_sem,
        device_id=device,
        device_id_type=pl.DeviceIdType.MESH,
    )


def greet(devices, conditions):
    barrier = pltpu.get_barrier_semaphore()
    for device, condition in zip(devices, conditions):

        @pl.when(condition)
        def _(device=device):
            pl.semaphore_signal(
                barrier, inc=1, device_id=device, device_id_type=pl.DeviceIdType.MESH
            )

    pl.semaphore_wait(barrier, sum(condition.astype(jnp.int32) for condition in conditions))


def expert_place():
    me = lax.axis_index("expert")
    return me, lax.div(me, 2), lax.rem(me, 2), lax.axis_size("expert") // 2


def line_partners():
    me, chip, core, chips = expert_place()
    band = lax.axis_index("dp")
    devices = [(band, me + 1 - 2 * core), (band, me + 2), (band, me - 2)]
    return devices, [chip >= 0, chip < chips - 1, chip > 0]


class Line:
    def __init__(self, own, slot, sems):
        self.own, self.slot = own, slot
        self.up_out, self.up_in, self.down_out, self.down_in, self.side_out, self.side_in, self.self_sem = sems
        self.me, self.chip, self.core, self.chips = expert_place()
        (self.twin, self.up, self.down), _ = line_partners()

    def local(self):
        return pltpu.make_async_copy(self.own, self.slot(self.me), self.self_sem)

    def side(self, source, block):
        return send_to(
            source,
            self.slot(2 * block + self.core),
            self.side_out.at[block],
            self.side_in.at[block],
            self.twin,
        )

    def upward(self, source, block, step):
        return send_to(
            source,
            self.slot(2 * block + self.core),
            self.up_out.at[step],
            self.up_in.at[step],
            self.up,
        )

    def downward(self, source, block, step):
        return send_to(
            source,
            self.slot(2 * block + self.core),
            self.down_out.at[step],
            self.down_in.at[step],
            self.down,
        )

    def begin(self):
        self.local().start()

        @pl.when(self.chip < self.chips - 1)
        def _():
            self.upward(self.own, self.chip, 0).start()

        @pl.when(self.chip > 0)
        def _():
            self.downward(self.own, self.chip, 0).start()

        self.side(self.own, self.chip).start()

    def advance(self, step):
        below, above = self.chip - 1 - step, self.chip + 1 + step

        @pl.when(below >= 0)
        def _():
            held = self.slot(2 * below + self.core)
            self.upward(held, below, step).wait_recv()

            if step + 1 < self.chips - 1:

                @pl.when(self.chip < self.chips - 1)
                def _():
                    self.upward(held, below, step + 1).start()

            self.side(held, below).start()

        @pl.when(above < self.chips)
        def _():
            held = self.slot(2 * above + self.core)
            self.downward(held, above, step).wait_recv()

            if step + 1 < self.chips - 1:

                @pl.when(self.chip > 0)
                def _():
                    self.downward(held, above, step + 1).start()

            self.side(held, above).start()

    def finish(self):
        self.local().wait()
        for step in range(self.chips - 1):

            @pl.when((self.chip < self.chips - 1) & (self.chip >= step))
            def _(step=step):
                block = self.chip - step
                self.upward(self.slot(2 * block + self.core), block, step).wait_send()

            @pl.when((self.chip > 0) & (self.chip + step < self.chips))
            def _(step=step):
                block = self.chip + step
                self.downward(self.slot(2 * block + self.core), block, step).wait_send()

        for block in range(self.chips):
            self.side(self.slot(2 * block + self.core), block).wait_send()
            send_to(
                self.slot(2 * block + self.core),
                self.slot(2 * block + 1 - self.core),
                self.side_out.at[block],
                self.side_in.at[block],
                self.twin,
            ).wait_recv()


def rows_kernel(own_ref, all_ref, *sems):
    greet(*line_partners())
    line = Line(own_ref, lambda i: all_ref.at[i], sems)
    line.begin()
    for step in range(line.chips - 1):
        line.advance(step)
    line.finish()


def gather_rows(own):
    peers = lax.axis_size("expert")
    anywhere = pl.BlockSpec(memory_space=pl.ANY)
    return pl.pallas_call(
        rows_kernel,
        out_shape=jax.ShapeDtypeStruct((peers, *own.shape), own.dtype),
        in_specs=[anywhere],
        out_specs=anywhere,
        scratch_shapes=line_sems(peers // 2),
        compiler_params=pltpu.CompilerParams(collective_id=1, has_side_effects=True),
    )(own)


def square_kernel(own_ref, all_ref, *sems):
    band, me = lax.axis_index("dp"), lax.axis_index("expert")
    outs, arrivals, twin_out, twin_in = sems[:3], sems[3:6], sems[6], sems[7]
    columns = [(band ^ 1, me), (band ^ 2, me)]
    devices, conditions = line_partners()
    greet(devices + columns, conditions + [band >= 0] * 2)
    line = Line(own_ref, lambda i: all_ref.at[band, i], sems[8:])
    chip, chips, core = line.chip, line.chips, line.core

    def across(source, block, step):
        return send_to(
            source,
            all_ref.at[band, 2 * block + core],
            outs[step - 1].at[block],
            arrivals[step - 1].at[block],
            (band ^ step, me),
        )

    def held(block, step):
        return all_ref.at[band ^ step, 2 * block + core]

    def arrive(block, step):
        send_to(
            own_ref,
            held(block, step),
            outs[step - 1].at[block],
            arrivals[step - 1].at[block],
            (band ^ step, me),
        ).wait_recv()

    def onward(block, step):
        return send_to(
            held(block, step),
            held(block, step),
            outs[2].at[block],
            arrivals[2].at[block],
            (band ^ (3 - step), me),
        )

    def twin(block, step):
        place = (step - 1) * chips + block
        return send_to(
            held(block, step),
            held(block, step),
            twin_out.at[place],
            twin_in.at[place],
            line.twin,
        )

    def spread(source, block):
        across(source, block, 1).start()
        across(source, block, 2).start()

    def receive(block):
        for step in (1, 2):
            arrive(block, step)

            @pl.when(lax.rem(block, 2) == step - 1)
            def _(step=step):
                onward(block, step).start()

            twin(block, step).start()

    line.begin()
    spread(own_ref, chip)
    for step in range(chips - 1):
        line.advance(step)
        below, above = chip - 1 - step, chip + 1 + step

        @pl.when(below >= 0)
        def _(below=below):
            spread(line.slot(2 * below + core), below)

        @pl.when(above < chips)
        def _(above=above):
            spread(line.slot(2 * above + core), above)

    receive(chip)
    for step in range(chips - 1):
        below, above = chip - 1 - step, chip + 1 + step

        @pl.when(below >= 0)
        def _(below=below):
            receive(below)

        @pl.when(above < chips)
        def _(above=above):
            receive(above)

    for block in range(chips):
        arrive(block, 3)
        twin(block, 3).start()
    line.finish()
    for block in range(chips):
        across(own_ref, block, 1).wait_send()
        across(own_ref, block, 2).wait_send()
        onward(block, 1).wait_send()
        for step in (1, 2, 3):
            place = (step - 1) * chips + block
            twin(block, step).wait_send()
            there = all_ref.at[band ^ step, 2 * block + 1 - core]
            send_to(there, there, twin_out.at[place], twin_in.at[place], line.twin).wait_recv()


def gather_square(own):
    bands, peers = lax.axis_size("dp"), lax.axis_size("expert")
    chips = peers // 2
    anywhere = pl.BlockSpec(memory_space=pl.ANY)
    return pl.pallas_call(
        square_kernel,
        out_shape=jax.ShapeDtypeStruct((bands, peers, *own.shape), own.dtype),
        in_specs=[anywhere],
        out_specs=anywhere,
        scratch_shapes=[pltpu.SemaphoreType.DMA((chips,))] * 6
        + [pltpu.SemaphoreType.DMA((3 * chips,))] * 2
        + line_sems(chips),
        compiler_params=pltpu.CompilerParams(collective_id=2, has_side_effects=True),
    )(own)


def start_kernel(
    tok_ref, pack_ref, wo_ref, tokens_ref, swap_ref, pack_all_ref, wo_all_ref, *sems
):
    bands, band = lax.axis_size("dp"), lax.axis_index("dp")
    me = lax.axis_index("expert")
    tok_out, tok_in, swap_out, swap_in, self_sems = sems[:5]
    pack_sems, wo_sems = sems[5:12], sems[12:]
    columns = [(band ^ step, me) for step in range(1, bands)]
    devices, conditions = line_partners()
    greet(devices + columns, conditions + [band >= 0] * (bands - 1))
    own_tok = pltpu.make_async_copy(tok_ref, tokens_ref.at[band], self_sems.at[0])
    own_swap = pltpu.make_async_copy(pack_ref.at[band], swap_ref.at[band], self_sems.at[1])
    own_swap.start()
    own_tok.start()

    def swap(step):
        other = band ^ step
        return send_to(
            pack_ref.at[other],
            swap_ref.at[band],
            swap_out.at[step - 1],
            swap_in.at[step - 1],
            (other, me),
        )

    def token(step):
        other = band ^ step
        return send_to(
            tok_ref, tokens_ref.at[band], tok_out.at[step - 1], tok_in.at[step - 1], (other, me)
        )

    def arrived(step, source, target, out, arrival):
        other = band ^ step
        send_to(
            source, target.at[other], out.at[step - 1], arrival.at[step - 1], (other, me)
        ).wait_recv()

    for step in range(1, bands):
        swap(step).start()
    wo_line = Line(wo_ref, lambda i: wo_all_ref.at[i], wo_sems)
    wo_line.begin()
    for step in range(1, bands):
        token(step).start()
    own_swap.wait()
    for step in range(1, bands):
        arrived(step, pack_ref.at[band], swap_ref, swap_out, swap_in)
    pack_line = Line(swap_ref, lambda i: pack_all_ref.at[:, i], pack_sems)
    pack_line.begin()
    for step in range(pack_line.chips - 1):
        wo_line.advance(step)
        pack_line.advance(step)
    wo_line.finish()
    pack_line.finish()
    own_tok.wait()
    for step in range(1, bands):
        arrived(step, tok_ref, tokens_ref, tok_out, tok_in)
        token(step).wait_send()
        swap(step).wait_send()


def start_moves(tokens, packed, w_output):
    bands, peers = lax.axis_size("dp"), lax.axis_size("expert")
    anywhere = pl.BlockSpec(memory_space=pl.ANY)
    chips = peers // 2
    shapes = [
        (bands, *tokens.shape),
        packed.shape,
        (bands, peers, *packed.shape[1:]),
        (peers, *w_output.shape),
    ]
    tokens_all, _, packed_all, output_all = pl.pallas_call(
        start_kernel,
        out_shape=[jax.ShapeDtypeStruct(shape, BF16) for shape in shapes],
        in_specs=[anywhere] * 3,
        out_specs=[anywhere] * 4,
        scratch_shapes=[pltpu.SemaphoreType.DMA((bands - 1,))] * 4
        + [pltpu.SemaphoreType.DMA((2,))]
        + line_sems(chips) * 2,
        compiler_params=pltpu.CompilerParams(collective_id=0, has_side_effects=True),
    )(tokens, packed, w_output)
    width = tokens.shape[1]
    return (
        tokens_all.reshape(-1, width),
        packed_all.reshape(-1, packed.shape[-1]),
        output_all.reshape(-1, width),
    )


def block_ranks(routes, peer, owned, experts):
    chosen = jnp.any(routes[..., None] == jnp.arange(experts, dtype=jnp.int32), axis=2)
    chosen = lax.dynamic_slice_in_dim(chosen, peer * owned, owned, axis=2)
    tok_count = chosen.shape[1]
    earlier = jnp.tril(jnp.ones((tok_count, tok_count), BF16), -1)
    ranks = dot("ts,bse->bet", earlier, chosen.astype(BF16)).astype(jnp.int32)
    return jnp.where(chosen.transpose(0, 2, 1), ranks, -1)


def slot_values(ranks, values):
    slots = jnp.arange(CAP, dtype=jnp.int32)
    chosen = ranks[:, :, None, :] == slots[None, None, :, None]
    return jnp.sum(jnp.where(chosen, values.transpose(0, 2, 1)[:, :, None, :], 0.0), axis=-1)


def by_core(values, core):
    paired = values.reshape(-1, 2, *values.shape[1:])
    return lax.dynamic_index_in_dim(paired, core, 1, keepdims=False)


def place_kernel(_, rank_ref, block_ref, rows_ref):
    count, owned, tok_count = rank_ref.shape
    slots = lax.broadcasted_iota(jnp.int32, (CAP, tok_count), 0)
    width = block_ref.shape[-1]
    for block in range(count):
        ranks = rank_ref[block]
        hot = jnp.concatenate([ranks[e : e + 1] == slots for e in range(owned)], axis=0)
        hot = jnp.where(hot, 1.0, 0.0).astype(BF16)
        for start in range(0, width, WIDTH_TILE):
            cols = slice(start, start + WIDTH_TILE)
            rows = jnp.dot(hot, block_ref[0, block, :, cols], preferred_element_type=F32)
            rows_ref[:, block, :, cols] = rows.astype(BF16).reshape(owned, CAP, WIDTH_TILE)


def place_rows(ranks, columns, first):
    total, owned, tok_count = ranks.shape
    peers = columns.shape[1]
    width = columns.shape[-1] - SIDE
    several = 2
    steps = peers // several

    def block_at(b, at):
        return lax.bitwise_xor(at[0], lax.div(b, steps)), lax.rem(b, steps), 0, 0

    return pl.pallas_call(
        place_kernel,
        grid_spec=pltpu.PrefetchScalarGridSpec(
            num_scalar_prefetch=1,
            grid=(total // several,),
            in_specs=[
                pl.BlockSpec((several, owned, tok_count), lambda b, at: (b, 0, 0)),
                pl.BlockSpec((1, several, tok_count, width), block_at),
            ],
            out_specs=pl.BlockSpec((owned, several, CAP, width), lambda b, at: (0, b, 0, 0)),
        ),
        out_shape=jax.ShapeDtypeStruct((owned, total, CAP, width), BF16),
        compiler_params=pltpu.CompilerParams(vmem_limit_bytes=VMEM_BYTES),
        cost_estimate=FREE,
    )(jnp.asarray(first, jnp.int32).reshape(1), ranks, columns)


def combine_kernel(rank_ref, rows_ref, out_ref):
    tok_count, owned = rank_ref.shape[1:]
    slots = owned * CAP
    width = out_ref.shape[-1]
    lane = lax.broadcasted_iota(jnp.int32, (tok_count, slots), 1)
    hot = jnp.zeros((tok_count, slots), F32)
    for e in range(owned):
        ranks = rank_ref[0, :, e : e + 1]
        hot = jnp.where((ranks >= 0) & (lane == ranks + e * CAP), 1.0, hot)
    hot = hot.astype(BF16)
    for start in range(0, width, WIDTH_TILE):
        cols = slice(start, start + WIDTH_TILE)
        rows = rows_ref[:, 0, :, cols].reshape(slots, WIDTH_TILE)
        out_ref[0, :, cols] = jnp.dot(hot, rows, preferred_element_type=F32).astype(BF16)


def combine(ranks, rows):
    count, tok_count, owned = ranks.shape
    width = rows.shape[-1]
    return pl.pallas_call(
        combine_kernel,
        grid=(count,),
        out_shape=jax.ShapeDtypeStruct((count, tok_count, width), BF16),
        in_specs=[
            pl.BlockSpec((1, tok_count, owned), lambda b: (b, 0, 0)),
            pl.BlockSpec((owned, 1, CAP, width), lambda b: (0, b, 0, 0)),
        ],
        out_specs=pl.BlockSpec((1, tok_count, width), lambda b: (b, 0, 0)),
        compiler_params=pltpu.CompilerParams(vmem_limit_bytes=VMEM_BYTES),
        cost_estimate=FREE,
    )(ranks, rows.reshape(owned, count, CAP, width))


def dot_nt(left, right):
    return lax.dot_general(left, right, (((1,), (1,)), ((), ())), preferred_element_type=F32)


def hidden_grads(x, c, gates, wg_ref, wu_ref, wd_ref):
    gate_in = jnp.dot(x, wg_ref[0], preferred_element_type=F32)
    up_in = jnp.dot(x, wu_ref[0], preferred_element_type=F32)
    raw = dot_nt(c, wd_ref[0])
    sig = 1.0 / (1.0 + jnp.exp(-gate_in))
    silu = gate_in * sig
    active = silu * up_in
    grad = raw * gates
    gate_grad = grad * up_in * (sig + silu * (1.0 - sig))
    up_grad = grad * silu
    return (active * gates).astype(BF16), gate_grad.astype(BF16), up_grad.astype(BF16), active * raw


def own_kernel(
    x_ref,
    c_ref,
    g_ref,
    wg_ref,
    wu_ref,
    wd_ref,
    active_ref,
    gate_ref,
    up_ref,
    slot_ref,
    back_ref,
    out_ref,
    back_sum,
    out_sum,
):
    width = x_ref.shape[-1]
    step = pl.program_id(2)
    active, gate_grad, up_grad, slot = hidden_grads(
        x_ref[0], c_ref[0], g_ref[0], wg_ref, wu_ref, wd_ref
    )
    active_ref[0] = active
    gate_ref[0] = gate_grad
    up_ref[0] = up_grad
    slot = jnp.sum(slot, axis=1, keepdims=True)
    slot_ref[0] = jnp.where(step == 0, slot, slot_ref[0] + slot)
    for start in range(0, width, WIDTH_TILE):
        cols = slice(start, start + WIDTH_TILE)
        rows = dot_nt(gate_ref[0], wg_ref[0, cols, :]) + dot_nt(up_ref[0], wu_ref[0, cols, :])
        back_sum[:, cols] = jnp.where(step == 0, rows, back_sum[:, cols] + rows)
        rows = jnp.dot(active_ref[0], wd_ref[0, :, cols], preferred_element_type=F32)
        out_sum[:, cols] = jnp.where(step == 0, rows, out_sum[:, cols] + rows)

    @pl.when(step == pl.num_programs(2) - 1)
    def _():
        back_ref[0] = back_sum[...].astype(BF16)
        out_ref[0] = out_sum[...].astype(BF16)


def own_experts(x_rows, c_rows, gates, rows, w_gate, w_up, w_down):
    owned, _, width = x_rows.shape
    hidden = w_down.shape[1]
    tile = HIDDEN_TILE
    some = min(rows, OWN_ROWS)
    whole = pl.BlockSpec((1, some, width), lambda e, r, f: (e, r, 0))
    column = pl.BlockSpec((1, some, 1), lambda e, r, f: (e, r, 0))
    part = pl.BlockSpec((1, some, tile), lambda e, r, f: (e, r, f))
    inward = pl.BlockSpec((1, width, tile), lambda e, r, f: (e, 0, f))
    outward = pl.BlockSpec((1, tile, width), lambda e, r, f: (e, f, 0))
    return pl.pallas_call(
        own_kernel,
        grid=(owned, rows // some, hidden // tile),
        in_specs=[whole, whole, column, inward, inward, outward],
        out_specs=[part, part, part, column, whole, whole],
        out_shape=[jax.ShapeDtypeStruct((owned, rows, hidden), BF16)] * 3
        + [jax.ShapeDtypeStruct((owned, rows, 1), F32)]
        + [jax.ShapeDtypeStruct((owned, rows, width), BF16)] * 2,
        scratch_shapes=[pltpu.VMEM((some, width), F32)] * 2,
        compiler_params=pltpu.CompilerParams(vmem_limit_bytes=VMEM_BYTES),
        cost_estimate=pl.CostEstimate(
            flops=12 * owned * rows * width * hidden,
            bytes_accessed=owned * (8 * rows * width + 6 * width * hidden),
            transcendentals=owned * rows * hidden,
        ),
    )(x_rows, c_rows, gates, w_gate, w_up, w_down)


def grads_kernel(
    x_ref, c_ref, g_ref, active_ref, gate_ref, up_ref, wg_ref, wu_ref, wd_ref, *rest
):
    dg_ref, du_ref, dd_ref, mark_ref, sums, pair, actives = rest[-7:]
    mark_ref[...] = jnp.zeros_like(mark_ref)
    tile = HIDDEN_TILE
    rows, width = x_ref.shape[1:]
    own = active_ref.shape[1]
    step = pl.program_id(1)

    def keep(start, active, gate_grad, up_grad):
        part = slice(start, start + own)
        actives[:, part] = active.T
        pair[:tile, part] = gate_grad.T
        pair[tile:, part] = up_grad.T

    def work_out(start):
        part = slice(start, start + own)
        active, gate_grad, up_grad, _ = hidden_grads(
            x_ref[0, part], c_ref[0, part], g_ref[0, part], wg_ref, wu_ref, wd_ref
        )
        keep(start, active, gate_grad, up_grad)

    @pl.when(step == 0)
    def _():
        keep(0, active_ref[0], gate_ref[0], up_ref[0])

    @pl.when(step > 0)
    def _():
        work_out(0)

    for start in range(own, rows, own):
        work_out(start)

    @pl.loop(0, width // WIDTH_TILE)
    def _(c):
        cols = pl.ds(pl.multiple_of(c * WIDTH_TILE, WIDTH_TILE), WIDTH_TILE)
        grads = jnp.dot(pair[...], x_ref[0, :, cols], preferred_element_type=F32)
        sums[:, cols] = jnp.where(step == 0, grads, sums[:, cols] + grads)
        grads = jnp.dot(actives[...], c_ref[0, :, cols], preferred_element_type=F32)
        dd_ref[0, :, cols] = jnp.where(step == 0, grads, dd_ref[0, :, cols] + grads)

    @pl.when(step == pl.num_programs(1) - 1)
    def _():
        same = lax.broadcasted_iota(jnp.int32, (tile, tile), 0) == lax.broadcasted_iota(
            jnp.int32, (tile, tile), 1
        )
        same = jnp.where(same, 1.0, 0.0).astype(BF16)

        @pl.loop(0, width // tile)
        def _(c):
            cols = pl.ds(pl.multiple_of(c * tile, tile), tile)
            dg_ref[0, cols, :] = dot_nt(same, sums[:tile, cols].astype(BF16))
            du_ref[0, cols, :] = dot_nt(same, sums[tile:, cols].astype(BF16))


def expert_grads(x_rows, c_rows, gates, own, w_gate, w_up, w_down, expert, buffers=None):
    owned, rows, width = x_rows.shape
    hidden = w_down.shape[1]
    tile, parts = HIDDEN_TILE, ROW_PARTS
    part, own_rows = rows // parts, own[0].shape[1]
    shapes = [(owned, width, hidden)] * 2 + [(owned, hidden, width)]
    in_specs = [
        pl.BlockSpec((1, part, width), lambda f, r: (expert, r, 0)),
        pl.BlockSpec((1, part, width), lambda f, r: (expert, r, 0)),
        pl.BlockSpec((1, part, 1), lambda f, r: (expert, r, 0)),
        *[pl.BlockSpec((1, own_rows, tile), lambda f, r: (expert, 0, f))] * 3,
        pl.BlockSpec((1, width, tile), lambda f, r: (expert, 0, f)),
        pl.BlockSpec((1, width, tile), lambda f, r: (expert, 0, f)),
        pl.BlockSpec((1, tile, width), lambda f, r: (expert, f, 0)),
    ]
    given = (x_rows, c_rows, gates, *own, w_gate, w_up, w_down)
    aliases = {}
    if buffers is not None:
        aliases = {len(given) + i: i for i in range(3)}
        in_specs += [pl.BlockSpec(memory_space=pl.ANY)] * 3
        given += tuple(buffers)
    return pl.pallas_call(
        grads_kernel,
        grid=(hidden // tile, parts),
        out_shape=[jax.ShapeDtypeStruct(shape, F32) for shape in [*shapes, (8, 128)]],
        in_specs=in_specs,
        out_specs=[
            pl.BlockSpec((1, width, tile), lambda f, r: (expert, 0, f)),
            pl.BlockSpec((1, width, tile), lambda f, r: (expert, 0, f)),
            pl.BlockSpec((1, tile, width), lambda f, r: (expert, f, 0)),
            pl.BlockSpec((8, 128), lambda f, r: (0, 0)),
        ],
        scratch_shapes=[
            pltpu.VMEM((2 * tile, width), F32),
            pltpu.VMEM((2 * tile, part), BF16),
            pltpu.VMEM((tile, part), BF16),
        ],
        input_output_aliases=aliases,
        compiler_params=pltpu.CompilerParams(vmem_limit_bytes=VMEM_BYTES),
        cost_estimate=pl.CostEstimate(
            flops=12 * rows * width * hidden,
            bytes_accessed=12 * rows * width + 24 * width * hidden,
            transcendentals=rows * hidden,
        ),
    )(*given)


def turn(values, cos, sin):
    return values * cos + pltpu.roll(values, values.shape[-1] // 2, 1) * sin


def qkv_kernel(
    tok_ref,
    gain_ref,
    w_ref,
    cos_ref,
    sin_ref,
    gq_ref,
    gk_ref,
    normed_ref,
    qpre_ref,
    kpre_ref,
    qrot_ref,
    krot_ref,
    value_ref,
):
    head = cos_ref.shape[1]
    heads = qpre_ref.shape[1] // head
    normed = norm_rows(tok_ref[...].astype(F32), gain_ref[...]).astype(BF16)
    normed_ref[...] = normed
    cos, sin = cos_ref[...], sin_ref[...]
    for pair in range(0, heads, 2):
        cols = slice(pair * head, (pair + 2) * head)
        pre = jnp.dot(normed, w_ref[:, cols], preferred_element_type=F32)
        qpre_ref[:, cols] = pre
        for h in range(2):
            one = slice(h * head, (h + 1) * head)
            rot = turn(norm_rows(pre[:, one], gq_ref[...]), cos, sin)
            qrot_ref[:, (pair + h) * head : (pair + h + 1) * head] = rot.astype(BF16)
    cols = slice(heads * head, (heads + 2) * head)
    pre = jnp.dot(normed, w_ref[:, cols], preferred_element_type=F32)
    kpre_ref[...] = pre[:, :head]
    krot_ref[...] = turn(norm_rows(pre[:, :head], gk_ref[...]), cos, sin).astype(BF16)
    value_ref[...] = pre[:, head:].astype(BF16)


def make_qkv(tokens, gain, weight, cos, sin, query_gain, key_gain):
    length, width = tokens.shape
    head = cos.shape[1]
    cols = weight.shape[1]
    q_cols = cols - 3 * head
    block = Q_BLOCK

    def rows(size):
        return pl.BlockSpec((block, size), lambda i: (i, 0))

    def fixed(*shape):
        return pl.BlockSpec(shape, lambda i: (0, 0))

    return pl.pallas_call(
        qkv_kernel,
        grid=(length // block,),
        in_specs=[
            rows(width),
            fixed(1, width),
            fixed(width, cols),
            rows(head),
            rows(head),
            fixed(1, head),
            fixed(1, head),
        ],
        out_specs=[rows(width), rows(q_cols), rows(head), rows(q_cols), rows(head), rows(head)],
        out_shape=[
            jax.ShapeDtypeStruct((length, width), BF16),
            jax.ShapeDtypeStruct((length, q_cols), F32),
            jax.ShapeDtypeStruct((length, head), F32),
            jax.ShapeDtypeStruct((length, q_cols), BF16),
            jax.ShapeDtypeStruct((length, head), BF16),
            jax.ShapeDtypeStruct((length, head), BF16),
        ],
        compiler_params=pltpu.CompilerParams(vmem_limit_bytes=VMEM_BYTES),
        cost_estimate=FREE,
    )(tokens, gain[None], weight, cos, sin, query_gain[None], key_gain[None])


def masked_scores(q_ref, k_ref, seg_row_ref, seg_col_ref, block, keys):
    size = q_ref.shape[0]
    scores = dot_nt(k_ref[:keys], q_ref[...]) * q_ref.shape[1] ** (-0.5)
    key_at = lax.broadcasted_iota(jnp.int32, (keys, size), 0)
    query_at = lax.broadcasted_iota(jnp.int32, (keys, size), 1) + block * size
    allowed = (key_at <= query_at) & (seg_col_ref[:keys] == seg_row_ref[...])
    return jnp.where(allowed, scores, -1e30)


def attend_kernel(q_ref, k_ref, vt_ref, seg_row_ref, seg_col_ref, out_ref, log_ref):
    size = q_ref.shape[0]
    blocks = k_ref.shape[0] // size
    for block in range(blocks):

        @pl.when(pl.program_id(1) == block)
        def _(block=block):
            keys = (block + 1) * size
            scores = masked_scores(q_ref, k_ref, seg_row_ref, seg_col_ref, block, keys)
            largest = jnp.max(scores, axis=0, keepdims=True)
            raised = jnp.exp(scores - largest)
            total = jnp.sum(raised, axis=0, keepdims=True)
            weights = (raised * (1.0 / total)).astype(BF16)
            out = jnp.dot(vt_ref[:, :keys], weights, preferred_element_type=F32)
            out_ref[...] = out.T.astype(BF16)
            log_ref[0] = largest + jnp.log(total)


def attend(query, key, value, segment):
    length, cols = query.shape
    head = key.shape[1]
    block = Q_BLOCK
    heads = cols // head
    return pl.pallas_call(
        attend_kernel,
        grid=(heads, length // block),
        in_specs=[
            pl.BlockSpec((block, head), lambda h, i: (i, h)),
            pl.BlockSpec((length, head), lambda h, i: (0, 0)),
            pl.BlockSpec((head, length), lambda h, i: (0, 0)),
            pl.BlockSpec((1, block), lambda h, i: (0, i)),
            pl.BlockSpec((length, 1), lambda h, i: (0, 0)),
        ],
        out_specs=[
            pl.BlockSpec((block, head), lambda h, i: (i, h)),
            pl.BlockSpec((1, 1, block), lambda h, i: (h, 0, i)),
        ],
        out_shape=[
            jax.ShapeDtypeStruct((length, cols), BF16),
            jax.ShapeDtypeStruct((heads, 1, length), F32),
        ],
        compiler_params=pltpu.CompilerParams(vmem_limit_bytes=VMEM_BYTES),
        cost_estimate=FREE,
    )(query, key, value.T, segment[None], segment[:, None])


def attend_back_kernel(
    q_ref,
    k_ref,
    kt_ref,
    v_ref,
    do_ref,
    log_ref,
    seg_row_ref,
    seg_col_ref,
    qpre_ref,
    kpre_ref,
    cos_ref,
    sin_ref,
    gq_ref,
    gk_ref,
    dq_ref,
    dk_ref,
    dv_ref,
    dgain_ref,
    key_sum,
    value_sum,
):
    size, head = q_ref.shape
    blocks = k_ref.shape[0] // size
    scale = head ** (-0.5)
    first = (pl.program_id(0) == 0) & (pl.program_id(1) == 0)
    last = (pl.program_id(0) == pl.num_programs(0) - 1) & (pl.program_id(1) == blocks - 1)

    @pl.when(first)
    def _():
        key_sum[...] = jnp.zeros_like(key_sum)
        value_sum[...] = jnp.zeros_like(value_sum)
        dgain_ref[...] = jnp.zeros_like(dgain_ref)

    def pull(grad, pre, gain, cos, sin):
        grad = grad.astype(BF16).astype(F32)
        turned = grad * cos + pltpu.roll(grad * sin, head // 2, 1)
        scale_row = lax.rsqrt(jnp.mean(pre * pre, axis=-1, keepdims=True) + EPSILON)
        unit = pre * scale_row
        gain_grad = jnp.sum(turned * unit, axis=0, keepdims=True)
        turned = turned * gain
        inner = jnp.mean(turned * unit, axis=-1, keepdims=True)
        return scale_row * (turned - unit * inner), gain_grad

    for block in range(blocks):

        @pl.when(pl.program_id(1) == block)
        def _(block=block):
            keys = (block + 1) * size
            rows = slice(block * size, keys)
            scores = masked_scores(q_ref, k_ref, seg_row_ref, seg_col_ref, block, keys)
            weights = jnp.exp(scores - log_ref[0])
            grads = dot_nt(v_ref[:keys], do_ref[...])
            inner = jnp.sum(weights * grads, axis=0, keepdims=True)
            score_grads = (weights * (grads - inner)).astype(BF16)
            value_sum[:keys] += jnp.dot(
                weights.astype(BF16), do_ref[...], preferred_element_type=F32
            )
            key_sum[:keys] += jnp.dot(score_grads, q_ref[...], preferred_element_type=F32)
            query_grad = jnp.dot(kt_ref[:, :keys], score_grads, preferred_element_type=F32)
            pre_grad, gain_grad = pull(
                query_grad.T * scale, qpre_ref[...], gq_ref[...], cos_ref[rows], sin_ref[rows]
            )
            dq_ref[...] = pre_grad.astype(BF16)
            dgain_ref[0:1] += gain_grad

    @pl.when(last)
    def _():
        pre_grad, gain_grad = pull(
            key_sum[...] * scale, kpre_ref[...], gk_ref[...], cos_ref[...], sin_ref[...]
        )
        dk_ref[...] = pre_grad.astype(BF16)
        dgain_ref[1:2] = gain_grad
        dv_ref[...] = value_sum[...].astype(BF16)


def attend_back(query, key, value, grad, logs, segment, qpre, kpre, cos, sin, gq, gk):
    length, cols = query.shape
    head = key.shape[1]
    block = Q_BLOCK
    heads = cols // head
    tile = pl.BlockSpec((block, head), lambda h, i: (i, h))

    def fixed(*shape):
        return pl.BlockSpec(shape, lambda h, i: (0, 0))

    return pl.pallas_call(
        attend_back_kernel,
        grid=(heads, length // block),
        in_specs=[
            tile,
            fixed(length, head),
            fixed(head, length),
            fixed(length, head),
            tile,
            pl.BlockSpec((1, 1, block), lambda h, i: (h, 0, i)),
            pl.BlockSpec((1, block), lambda h, i: (0, i)),
            fixed(length, 1),
            tile,
            fixed(length, head),
            fixed(length, head),
            fixed(length, head),
            fixed(1, head),
            fixed(1, head),
        ],
        out_specs=[tile, fixed(length, head), fixed(length, head), fixed(8, head)],
        out_shape=[
            jax.ShapeDtypeStruct((length, cols), BF16),
            jax.ShapeDtypeStruct((length, head), BF16),
            jax.ShapeDtypeStruct((length, head), BF16),
            jax.ShapeDtypeStruct((8, head), F32),
        ],
        scratch_shapes=[pltpu.VMEM((length, head), F32), pltpu.VMEM((length, head), F32)],
        compiler_params=pltpu.CompilerParams(vmem_limit_bytes=VMEM_BYTES),
        cost_estimate=FREE,
    )(
        query,
        key,
        key.T,
        value,
        grad,
        logs,
        segment[None],
        segment[:, None],
        qpre,
        kpre,
        cos,
        sin,
        gq[None],
        gk[None],
    )


def on_device(
    tokens,
    segment_ids,
    routes,
    w_query,
    w_key,
    w_value,
    w_output,
    w_router,
    gain_attn,
    gain_moe,
    gain_query,
    gain_key,
    w_gate,
    w_up,
    w_down,
    cotangent,
):
    bands, peers = lax.axis_size("dp"), lax.axis_size("expert")
    band, peer = lax.axis_index("dp"), lax.axis_index("expert")
    own_tokens = tokens[0]
    tok_count, width = own_tokens.shape
    band_rows = w_query.shape[0]
    experts = w_router.shape[1]
    gain_rows = gain_query.shape[0]
    head_size = gain_rows * bands * peers
    heads = w_query.shape[1] // head_size // bands
    q_cols, k_cols = heads * head_size, head_size
    qkv_cols = q_cols + 2 * k_cols
    owned = experts // peers

    small = jnp.concatenate(
        [
            w_router,
            gain_attn[:, None],
            gain_moe[:, None],
            jnp.pad(gain_query, (0, band_rows - gain_rows))[:, None],
            jnp.pad(gain_key, (0, band_rows - gain_rows))[:, None],
        ],
        axis=1,
    )
    small = jnp.pad(small, ((0, 0), (0, 128 - small.shape[1])))
    packed = jnp.concatenate(
        [
            w_query.reshape(band_rows, bands, q_cols),
            w_key.reshape(band_rows, bands, k_cols),
            w_value.reshape(band_rows, bands, k_cols),
            jnp.broadcast_to(small[:, None], (band_rows, bands, 128)),
        ],
        axis=-1,
    ).transpose(1, 0, 2)
    tokens_all, packed_all, out_w = start_moves(own_tokens, packed, w_output)
    qkv_w = packed_all[:, :qkv_cols]
    small_all = packed_all[:, qkv_cols:]
    router_full = small_all[:, :experts]
    attn_gain = small_all[:, experts].astype(F32)
    moe_gain = small_all[:, experts + 1].astype(F32)
    head_gains = small_all.reshape(bands * peers, band_rows, 128)[:, :gain_rows]
    query_gain = head_gains[:, :, experts + 2].reshape(-1).astype(F32)
    key_gain = head_gains[:, :, experts + 3].reshape(-1).astype(F32)
    shared = owned >= bands == 4
    top = routes.shape[-1]

    def beside(rows, *sides):
        used = sum(side.shape[-1] for side in sides)
        filler = jnp.zeros((tok_count, SIDE - used), BF16)
        return jnp.concatenate([rows, *(side.astype(BF16) for side in sides), filler], axis=1)

    def side_gates(sides):
        gates = sides[..., :experts].astype(F32)
        gates = gates + sides[..., experts : 2 * experts].astype(F32)
        return lax.dynamic_slice_in_dim(gates, peer * owned, owned, axis=2)

    cot_rows = beside(after(cotangent[0], out_w), routes[0])
    if shared:
        cot_all = lax.all_gather(cot_rows, ("dp", "expert"), axis=0, tiled=False)
        cot_all = cot_all.reshape(bands, peers, tok_count, -1)
    else:
        cot_all = lax.all_gather(cot_rows, "expert", axis=0)[None]
    here = band if shared else 0

    inputs = own_tokens.astype(F32)
    length = tokens_all.shape[0]
    half = head_size // 2
    frequency = ROPE_BASE ** (-jnp.arange(half, dtype=F32) * 2.0 / head_size)
    angles = jnp.arange(length, dtype=jnp.int32).astype(F32)[:, None] * frequency[None, :]
    cos = jnp.concatenate([jnp.cos(angles)] * 2, axis=-1)
    sin = jnp.concatenate([-jnp.sin(angles), jnp.sin(angles)], axis=-1)
    normed, query_pre, key_pre, query_low, key_low, value_low = make_qkv(
        tokens_all, attn_gain, packed_all, cos, sin, query_gain, key_gain
    )
    segment = segment_ids[0]
    attended_low, log_total = attend(query_low, key_low, value_low, segment)
    branch = dot("tm,md->td", attended_low, out_w).astype(BF16)
    branch = sum_blocks(branch.reshape(bands, tok_count, width), "dp")
    hidden = inputs + branch

    normed_moe_f, moe_pull = jax.vjp(norm_rows, hidden, moe_gain)
    normed_moe = normed_moe_f.astype(BF16)
    mask = jnp.any(routes[0][..., None] == jnp.arange(experts, dtype=jnp.int32), axis=1)
    own_gates = masked_softmax(dot("td,de->te", normed_moe, router_full), mask)
    high = own_gates.astype(BF16)
    low = own_gates - high.astype(F32)
    moe_rows = beside(normed_moe, high, low)
    moe_all = gather_square(moe_rows) if shared else gather_rows(moe_rows)[None]
    cot_all = after(cot_all, moe_all)

    def in_order(columns):
        pick = [
            lax.dynamic_index_in_dim(columns, here ^ i, 0, keepdims=False)
            for i in range(len(columns))
        ]
        return jnp.concatenate(pick)

    routes_all = in_order(cot_all[..., width : width + top]).astype(jnp.int32)
    ranks_all = block_ranks(routes_all, peer, owned, experts)
    own_ranks = ranks_all[:peers]
    token_ranks = own_ranks.transpose(0, 2, 1)
    cot_placed = place_rows(ranks_all, cot_all, here).reshape(owned, -1, width)
    x_placed = place_rows(ranks_all, moe_all, here).reshape(owned, -1, width)
    all_gates = slot_values(ranks_all, side_gates(in_order(moe_all[..., width:])))
    all_gates = all_gates.transpose(1, 0, 2).reshape(owned, -1, 1)
    *own, slot_grads, rows_back, rows_out = own_experts(
        x_placed,
        cot_placed,
        all_gates,
        peers * CAP,
        w_gate,
        w_up,
        w_down,
    )
    if not shared:
        active, gate_low, up_low = own
        expert_sums = lax.psum(
            (
                dot("erd,erf->edf", x_placed, gate_low).astype(BF16),
                dot("erd,erf->edf", x_placed, up_low).astype(BF16),
                dot("erf,erd->efd", active, cot_placed).astype(BF16),
            ),
            "dp",
        )
    rows_back = combine(token_ranks, rows_back)
    back = lax.psum_scatter(rows_back, "expert", scatter_dimension=0, tiled=True)[0]
    slot_grads = slot_grads.reshape(owned, peers, CAP).transpose(1, 0, 2)
    slots = jnp.arange(CAP, dtype=jnp.int32)[None, None, :, None]
    token_grads = jnp.where(own_ranks[:, :, None, :] == slots, slot_grads[..., None], 0.0)
    token_grads = jnp.sum(token_grads, axis=2)
    gate_grads = (
        lax.all_to_all(token_grads, "expert", split_axis=0, concat_axis=0, tiled=True)
        .reshape(experts, tok_count)
        .T
    )
    rows_out = combine(after(token_ranks, rows_back), rows_out)

    expert_sums = None if shared else expert_sums

    def next_expert(number, sums, *earlier):
        if not shared or number >= owned:
            return sums, earlier[0]
        *sums, mark = expert_grads(
            x_placed,
            cot_placed,
            after(all_gates, *earlier),
            own,
            w_gate,
            w_up,
            w_down,
            number,
            sums,
        )
        return sums, mark

    expert_sums, mark = next_expert(0, expert_sums, rows_out)
    back = after(back, mark)

    grad_logits = own_gates * (
        gate_grads - jnp.sum(own_gates * gate_grads, axis=-1, keepdims=True)
    )
    grad_router_w = jnp.einsum("td,te->de", normed_moe.astype(F32), grad_logits, precision=PRECISE)
    grad_normed = back.astype(F32) + jnp.einsum(
        "te,de->td", grad_logits, router_full.astype(F32), precision=PRECISE
    )
    grad_hidden_n, grad_moe_gain = moe_pull(grad_normed)
    grad_hidden = cotangent[0].astype(F32) + grad_hidden_n
    grad_branch = grad_hidden.astype(BF16)
    branch_all = lax.all_gather(grad_branch, "dp", axis=0, tiled=True)
    expert_sums, mark = next_expert(1, expert_sums, grad_branch)
    branch_all = after(branch_all, mark)

    grad_attended = dot("td,md->tm", branch_all, out_w).astype(BF16)
    query_grad, key_grad, value_grad, head_grads = attend_back(
        query_low,
        key_low,
        value_low,
        grad_attended,
        log_total,
        segment,
        query_pre,
        key_pre,
        cos,
        sin,
        query_gain,
        key_gain,
    )
    qkv_grad = jnp.concatenate([query_grad, key_grad, value_grad], axis=1)
    grad_normed_attn = dot("tm,dm->td", qkv_grad, qkv_w).astype(BF16)
    expert_sums, mark = next_expert(2, expert_sums, grad_normed_attn)
    grad_normed_attn = lax.psum_scatter(
        grad_normed_attn, "dp", scatter_dimension=0, tiled=True
    )
    grad_normed_attn = after(grad_normed_attn, mark).astype(F32)
    _, attn_pull = jax.vjp(norm_rows, inputs, attn_gain)
    grad_inputs_n, grad_attn_gain = attn_pull(grad_normed_attn)
    grad_tokens = grad_hidden + grad_inputs_n

    whole_gains = jnp.stack([grad_attn_gain, grad_moe_gain], axis=1)
    head_gains = head_grads[:2].T
    head_gains = jnp.pad(
        head_gains.reshape(bands * peers, gain_rows, 2),
        ((0, 0), (0, band_rows - gain_rows), (0, 0)),
    )
    small_grad = jnp.concatenate(
        [grad_router_w, whole_gains, head_gains.reshape(width, 2)], axis=1
    )
    small_grad = jnp.pad(small_grad, ((0, 0), (0, 128 - small_grad.shape[1])))
    band_qkv = jnp.concatenate([dot("td,tm->dm", normed, qkv_grad), small_grad], axis=1)
    band_qkv = band_qkv.astype(BF16).reshape(bands, peers, band_rows, -1).transpose(1, 0, 2, 3)
    for number in range(3, owned):
        expert_sums, mark = next_expert(number, expert_sums, band_qkv)
    band_qkv = lax.psum_scatter(
        band_qkv.reshape(width, -1), "expert", scatter_dimension=0, tiled=True
    ).reshape(bands, band_rows, -1)
    band_qkv = after(band_qkv, mark)
    band_qkv = lax.all_to_all(band_qkv, "dp", split_axis=0, concat_axis=0, tiled=True).transpose(
        1, 0, 2
    )
    grad_query = band_qkv[:, :, :q_cols].astype(F32).reshape(band_rows, -1)
    grad_key = band_qkv[:, :, q_cols : q_cols + k_cols].astype(F32).reshape(band_rows, -1)
    grad_value = band_qkv[:, :, q_cols + k_cols : qkv_cols].astype(F32).reshape(band_rows, -1)
    smaller = jnp.sum(band_qkv[:, :, qkv_cols:].astype(F32), axis=1)
    grad_output = sum_peers(
        dot("tm,td->md", attended_low, branch_all).astype(BF16).reshape(peers, -1, width)
    )

    moe_sum = sum_peers(after(rows_out, branch_all))
    block_out = (hidden + moe_sum).astype(BF16)
    return (
        block_out[None],
        grad_tokens[None],
        grad_query,
        grad_key,
        grad_value,
        grad_output,
        smaller[:, :experts],
        smaller[:, experts],
        smaller[:, experts + 1],
        smaller[:gain_rows, experts + 2],
        smaller[:gain_rows, experts + 3],
        expert_sums[0].astype(F32),
        expert_sums[1].astype(F32),
        expert_sums[2].astype(F32),
    )


def solution(mesh):
    both = ("dp", "expert")
    return jax.shard_map(
        on_device,
        mesh=mesh,
        in_specs=(
            P("expert", "dp", None),
            P("expert", None),
            P("expert", "dp", None),
            P(both, None),
            P(both, None),
            P(both, None),
            P(both, None),
            P(both, None),
            P(both),
            P(both),
            P(both),
            P(both),
            P("expert", None, None),
            P("expert", None, None),
            P("expert", None, None),
            P("expert", "dp", None),
        ),
        out_specs=(
            P("expert", "dp", None),
            P("expert", "dp", None),
            P(both, None),
            P(both, None),
            P(both, None),
            P(both, None),
            P(both, None),
            P(both),
            P(both),
            P(both),
            P(both),
            P("expert", None, None),
            P("expert", None, None),
            P("expert", None, None),
        ),
        check_vma=False,
    )
```

profile of v0, /device:TPU:0, one launch (start us, length us, event | category | flops | bytes accessed | tf_op | source)
XLA Modules:
  0.0 1220.2 jit_solution(305190722764417557)
XLA Ops:
  11.4 2.3 copy.253.refs_0_
  14.7 89.0 %shard_map.263 = (bf16[4,256,2048]{2,1,0:T(8,128)(2,1)}, bf16[4,64,1408]{2,1,0:T(8,128)(2,1)}, bf16[4,8,64,1408]{3,2,1,0:T(8,128)(2,1)}, bf16[8,128,2048]{2,1,0:T(8,128)(2,1)}) custom-call(bf16[256,2048]{1,0:T(8,128)(2,1)} %bitcast.195, bf16[4,64,1408]{2,1,0:T(8,128)(2,1)} %maximum_bitcast_fusion.pack_ref, bf16[128,2048]{1,0:T(8,128)(2,1)} %wo_ref.1), custom_call_target="tpu_custom_call" | custom-call | tf_op jit(solution)/shard_map/pallas_call | solution.py:460
  103.8 3.0 concatenate.56
  111.0 1.9 fusion.29
  114.2 2.7 convert_reduce_fusion
  117.0 13.1 %shard_map.264 = (bf16[1024,2048]{1,0:T(8,128)(2,1)}, f32[1024,1024]{1,0:T(8,128)}, f32[1024,128]{1,0:T(8,128)}, bf16[1024,1024]{1,0:T(8,128)(2,1)}, bf16[1024,1...) custom-call(bf16[1024,2048]{1,0:T(8,128)(2,1)} %bitcast.211, f32[1,2048]{1,0:T(1,128)} %bitcast.225, ...), custom_call_target="tpu_custom_call" | custom-call | tf_op jit(solution)/shard_map/pallas_call | solution.py:811
  130.1 1.8 copy.188
  131.9 29.7 %shard_map.265 = (bf16[1024,1024]{1,0:T(8,128)(2,1)}, f32[8,1,1024]{2,1,0:T(1,128)}) custom-call(bf16[1024,1024]{1,0:T(8,128)(2,1)} %get-tuple-element.53.q_ref, bf16[1024,128]{1,0:T(8,128)(2,1)} %get-tuple-element.54.k_ref, bf16[128,1024]{1,0:T(8,128)(2,1)} %bitcast.219, s32[1,1024]{1,0:T(1,128)} %seg_row_ref.3, s32[1024,1]{1,0:T(8,128)} %copy.189.seg_col_ref), custom_call_target="tpu_custom_call" | custom-call | tf_op jit(solution)/shard_map/pallas_call | solution.py:869
  161.6 7.3 convolution_convert_fusion.2
  175.6 29.4 %collective-permute-done = bf16[256,2048]{1,0:T(8,128)(2,1)S(1)} collective-permute-done((bf16[256,2048]{1,0:T(8,128)(2,1)}, bf16[256,2048]{1,0:T(8,128)(2,1)S(1)}, u32[]{:S(2)}, u32[]{:S(2)}) %collective-permute-start) | collective-permute-done | bytes 1048608 | tf_op jit(solution)/shard_map/ppermute | solution.py:64
  205.0 29.5 %collective-permute-done.2 = bf16[256,2048]{1,0:T(8,128)(2,1)S(1)} collective-permute-done((bf16[256,2048]{1,0:T(8,128)(2,1)}, bf16[256,2048]{1,0:T(8,128)(2,1)S(1)}, u32[]{:S(2)}, u32[]{:S(2)}) %collective-permute-start.2) | collective-permute-done | bytes 1048608 | tf_op jit(solution)/shard_map/ppermute | solution.py:64
  234.5 3.0 multiply_reduce_fusion.2
  239.2 1.9 select_reduce_fusion.2
  242.2 1.9 concatenate.57.own_ref
  244.1 225.0 %shard_map.267.refs_1_.block_ref = bf16[4,8,256,2176]{3,2,1,0:T(8,128)(2,1)} custom-call(bf16[256,2176]{1,0:T(8,128)(2,1)} %concatenate.57.own_ref), custom_call_target="tpu_custom_call" | custom-call | tf_op jit(solution)/shard_map/pallas_call | solution.py:378
  471.9 3.2 add_bitcast_fusion
  475.1 3.0 copy.204
  480.8 2.8 fusion.1
  483.7 1.7 copy.229
  485.7 2.7 copy.200
  488.4 5.0 convert_select_fusion
  493.4 3.5 copy.201.rank_ref
  496.9 2.4 fusion.49
  499.3 33.5 %shard_map.270 = bf16[4,32,80,2048]{3,2,1,0:T(8,128)(2,1)} custom-call(s32[1]{0:T(128)} %bitcast.28._, s32[32,4,256]{2,1,0:T(4,128)} %copy.201.rank_ref, bf16[4,8,256,2176]{3,2,1,0:T(8,128)(2,1)} %shard_map.268.block_ref), custom_call_target="tpu_custom_call" | custom-call | tf_op jit(solution)/shard_map/pallas_call | solution.py:522
  532.8 33.6 %shard_map.269 = bf16[4,32,80,2048]{3,2,1,0:T(8,128)(2,1)} custom-call(s32[1]{0:T(128)} %bitcast.28._, s32[32,4,256]{2,1,0:T(4,128)} %copy.201.rank_ref, bf16[4,8,256,2176]{3,2,1,0:T(8,128)(2,1)} %shard_map.267.refs_1_.block_ref), custom_call_target="tpu_custom_call" | custom-call | tf_op jit(solution)/shard_map/pallas_call | solution.py:522
  566.4 2.3 select_reduce_fusion
  568.7 4.1 reshape.315.g_ref.refs_0_
  572.8 77.2 %shard_map.271 = (bf16[4,640,768]{2,1,0:T(8,128)(2,1)}, bf16[4,640,768]{2,1,0:T(8,128)(2,1)}, bf16[4,640,768]{2,1,0:T(8,128)(2,1)}, f32[4,640,1]{2,1,0:T(8,128)}...) custom-call(bf16[4,2560,2048]{2,1,0:T(8,128)(2,1)} %bitcast.184, bf16[4,2560,2048]{2,1,0:T(8,128)(2,1)} %bitcast.179, ...), custom_call_target="tpu_custom_call" | custom-call | flops 48318382080 | bytes 79691776 | tf_op jit(solution)/shard_map/pallas_call | solution.py:638
  650.0 13.4 %shard_map.272.refs_1_ = bf16[8,256,2048]{2,1,0:T(8,128)(2,1)} custom-call(s32[8,256,4]{2,1,0:T(8,128)} %get-tuple-element.151.rank_ref.refs_0_, bf16[4,8,80,2048]{3,2,1,0:T(8,128)(2,1)} %bitcast.203), custom_call_target="tpu_custom_call" | custom-call | tf_op jit(solution)/shard_map/pallas_call | solution.py:558
  663.5 5.4 copy.271.refs_0_
  668.8 2.3 copy.265.refs_0_
  671.2 2.3 copy.258.refs_0_
  676.7 6.9 all-to-all-start
  683.7 13.9 %shard_map.274.refs_1_.refs_0_ = bf16[8,256,2048]{2,1,0:T(8,128)(2,1)} custom-call(s32[8,256,4]{2,1,0:T(8,128)} %shard_map.273.rank_ref, bf16[4,8,80,2048]{3,2,1,0:T(8,128)(2,1)} %bitcast.202), custom_call_target="tpu_custom_call" | custom-call | tf_op jit(solution)/shard_map/pallas_call | solution.py:558
  697.6 67.0 %shard_map.276 = (f32[4,2048,768]{2,1,0:T(8,128)}, f32[4,2048,768]{2,1,0:T(8,128)}, f32[4,768,2048]{2,1,0:T(8,128)}, f32[8,128]{1,0:T(8,128)}) custom-call(bf16[4,2560,2048]{2,1,0:T(8,128)(2,1)} %bitcast.185, bf16[4,2560,2048]{2,1,0:T(8,128)(2,1)} %bitcast.180, f32[4,2560,1]{2,1,0:T(8,128)} %shard_map.275.g_ref, ...), custom_call_target="tpu_custom_call" | custom-call | flops 48318382080 | bytes 100663296 | tf_op jit(solution)/shard_map/pallas_call | solution.py:733
  766.2 3.1 multiply_reduce_fusion
  770.6 1.7 fusion.47.refs_1_
  773.3 67.0 %shard_map.279 = (f32[4,2048,768]{2,1,0:T(8,128)}, f32[4,2048,768]{2,1,0:T(8,128)}, f32[4,768,2048]{2,1,0:T(8,128)}, f32[8,128]{1,0:T(8,128)}) custom-call(bf16[4,2560,2048]{2,1,0:T(8,128)(2,1)} %bitcast.186, bf16[4,2560,2048]{2,1,0:T(8,128)(2,1)} %bitcast.181, ...), custom_call_target="tpu_custom_call", output_to_operand_aliasing={{0}: (9, {}), {1}: (10, {}), {2}: (11, {})} | custom-call | flops 48318382080 | bytes 100663296 | tf_op jit(solution)/shard_map/pallas_call | solution.py:733
  840.4 9.3 convolution_convert_fusion.4.do_ref
  849.6 38.4 %shard_map.282 = (bf16[1024,1024]{1,0:T(8,128)(2,1)}, bf16[1024,128]{1,0:T(8,128)(2,1)}, bf16[1024,128]{1,0:T(8,128)(2,1)}, f32[8,128]{1,0:T(8,128)}) custom-call(bf16[1024,1024]{1,0:T(8,128)(2,1)} %get-tuple-element.53.q_ref, bf16[1024,128]{1,0:T(8,128)(2,1)} %get-tuple-element.54.k_ref, bf16[128,1024]{1,0:T(8,128)(2,1)} %bitcast.218, ...), custom_call_target="tpu_custom_call" | custom-call | tf_op jit(solution)/shard_map/pallas_call | solution.py:978
  888.0 1.8 constant_dynamic-update-slice_fusion.2
  891.5 9.6 fusion.5.refs_1_
  904.8 11.2 convolution_convert_fusion
  916.0 67.3 %shard_map.284 = (f32[4,2048,768]{2,1,0:T(8,128)}, f32[4,2048,768]{2,1,0:T(8,128)}, f32[4,768,2048]{2,1,0:T(8,128)}, f32[8,128]{1,0:T(8,128)}) custom-call(bf16[4,2560,2048]{2,1,0:T(8,128)(2,1)} %bitcast.187, bf16[4,2560,2048]{2,1,0:T(8,128)(2,1)} %bitcast.182, ...), custom_call_target="tpu_custom_call", output_to_operand_aliasing={{0}: (9, {}), {1}: (10, {}), {2}: (11, {})} | custom-call | flops 48318382080 | bytes 100663296 | tf_op jit(solution)/shard_map/pallas_call | solution.py:733
  984.5 2.3 fusion.9
  987.3 8.4 copy_bitcast_fusion.5
  995.8 4.9 dynamic-slice_bitcast_fusion
  1001.0 5.0 convolution_convert_fusion.1
  1006.0 1.9 copy-done.13
  1008.5 4.1 collective-permute-done.7
  1012.6 3.0 fusion.4
  1016.8 1.8 collective-permute-start.8
  1018.6 2.0 collective-permute-start.10
  1021.6 23.4 %collective-permute-done.8 = bf16[128,2048]{1,0:T(8,128)(2,1)} collective-permute-done((bf16[128,2048]{1,0:T(8,128)(2,1)}, bf16[128,2048]{1,0:T(8,128)(2,1)}, u32[]{:S(2)}, u32[]{:S(2)}) %collective-permute-start.8) | collective-permute-done | bytes 524320 | tf_op jit(solution)/shard_map/ppermute | solution.py:60
  1045.0 18.3 %collective-permute-done.10 = bf16[128,2048]{1,0:T(8,128)(2,1)} collective-permute-done((bf16[128,2048]{1,0:T(8,128)(2,1)}, bf16[128,2048]{1,0:T(8,128)(2,1)}, u32[]{:S(2)}, u32[]{:S(2)}) %collective-permute-start.10) | collective-permute-done | bytes 524320 | tf_op jit(solution)/shard_map/ppermute | solution.py:60
  1063.2 34.0 %collective-permute-done.9 = bf16[128,2048]{1,0:T(8,128)(2,1)} collective-permute-done((bf16[128,2048]{1,0:T(8,128)(2,1)}, bf16[128,2048]{1,0:T(8,128)(2,1)}, u32[]{:S(2)}, u32[]{:S(2)}) %collective-permute-start.9) | collective-permute-done | bytes 524320 | tf_op jit(solution)/shard_map/ppermute | solution.py:60
  1097.2 2.6 fusion.23
  1099.9 5.4 fusion
  1105.3 1.8 dynamic-slice_bitcast_fusion.4
  1108.3 3.8 collective-permute-start.6
  1112.1 66.8 %shard_map.287 = (f32[4,2048,768]{2,1,0:T(8,128)}, f32[4,2048,768]{2,1,0:T(8,128)}, f32[4,768,2048]{2,1,0:T(8,128)}, f32[8,128]{1,0:T(8,128)}) custom-call(bf16[4,2560,2048]{2,1,0:T(8,128)(2,1)} %bitcast.188, bf16[4,2560,2048]{2,1,0:T(8,128)(2,1)} %bitcast.183, ...), custom_call_target="tpu_custom_call", output_to_operand_aliasing={{0}: (9, {}), {1}: (10, {}), {2}: (11, {})} | custom-call | flops 48318382080 | bytes 100663296 | tf_op jit(solution)/shard_map/pallas_call | solution.py:733
  1179.0 4.3 all-to-all-start.1
  1183.4 17.2 %collective-permute-done.5 = bf16[256,2048]{1,0:T(8,128)(2,1)} collective-permute-done((bf16[256,2048]{1,0:T(8,128)(2,1)}, bf16[256,2048]{1,0:T(8,128)(2,1)}, u32[]{:S(2)}, u32[]{:S(2)}) %collective-permute-start.5) | collective-permute-done | bytes 1048608 | tf_op jit(solution)/shard_map/ppermute | solution.py:60
  1200.6 5.5 fusion.12
  (209 shorter events, 51.4 us)
Async XLA Ops:
  7.2 6.5 copy-start
  7.2 6.5 copy-start.27
  7.2 470.9 %all-gather.6.cloned.1.call-start = ((), (), s32[]{:S(2)}) async-start(), calls=%async_computation.9 | async-start | bytes 36765696 | tf_op jit(solution)/shard_map/all_gather | solution.py:1100
  103.7 3.1 copy-start.28
  106.8 658.1 %reduce-scatter.4.cloned.1.call-start = ((), (), s32[]{:S(2)}) async-start(), calls=%async_computation.5 | async-start | bytes 9437184 | tf_op jit(solution)/shard_map/reduce_scatter | solution.py:1167
  117.0 120.5 %copy-start.23 = (f32[2048]{0:T(1024)}, f32[2048]{0:T(1024)S(1)}, u32[]{:S(2)}) copy-start(f32[2048]{0:T(1024)S(1)} %get-tuple-element.130) | copy-start | bytes 24580
  168.9 3.0 copy-start.14
  169.0 6.4 copy-start.29
  169.0 65.5 %copy-start.10 = (bf16[1,256,2048]{2,1,0:T(8,128)(2,1)S(1)}, bf16[1,256,2048]{2,1,0:T(8,128)(2,1)}, u32[]{:S(2)}) copy-start(bf16[1,256,2048]{2,1,0:T(8,128)(2,1)} %param.16) | copy-start | bytes 3145732
  171.9 33.1 %collective-permute-start = (bf16[256,2048]{1,0:T(8,128)(2,1)}, bf16[256,2048]{1,0:T(8,128)(2,1)S(1)}, u32[]{:S(2)}, u32[]{:S(2)}) collective-permute-start(bf16[256,2048]{1,0:T(8,128)(2,1)} %get-tuple-element.152), channel_id=1, source_target_pairs={{0,8},{8,0},{16,24},{24,16},{1,9},{9,1},{17,25},{25,17},{2,10},{10... | collective-permute-start | bytes 3145736 | tf_op jit(solution)/shard_map/ppermute | solution.py:64
  172.7 61.7 %collective-permute-start.2 = (bf16[256,2048]{1,0:T(8,128)(2,1)}, bf16[256,2048]{1,0:T(8,128)(2,1)S(1)}, u32[]{:S(2)}, u32[]{:S(2)}) collective-permute-start(bf16[256,2048]{1,0:T(8,128)(2,1)} %get-tuple-element.153), channel_id=1, source_target_pairs={{0,24},{8,16},{16,8},{24,0},{1,25},{9,17},{17,9},{25,1},{2,26},{10... | collective-permute-start | bytes 3145736 | tf_op jit(solution)/shard_map/ppermute | solution.py:64
  174.2 60.3 %collective-permute-start.1 = (bf16[256,2048]{1,0:T(8,128)(2,1)}, bf16[256,2048]{1,0:T(8,128)(2,1)}, u32[]{:S(2)}, u32[]{:S(2)}) collective-permute-start(bf16[256,2048]{1,0:T(8,128)(2,1)} %get-tuple-element.154), channel_id=1, source_target_pairs={{0,16},{8,24},{16,0},{24,8},{1,17},{9,25},{17,1},{25,9},{2,18},{10... | collective-permute-start | bytes 3145736 | tf_op jit(solution)/shard_map/ppermute | solution.py:64
  237.5 1.4 copy-start.2
  237.5 3.5 copy-start.37
  237.5 3.5 copy-start.30
  239.1 4.9 copy-start.7
  469.0 1.6 slice-start
  532.8 33.6 %copy-start.16 = (s32[32,4,256]{2,1,0:T(4,128)S(1)}, s32[32,4,256]{2,1,0:T(4,128)}, u32[]{:S(2)}) copy-start(s32[32,4,256]{2,1,0:T(4,128)} %copy.201.rank_ref) | copy-start | bytes 393220
  663.4 5.4 slice-start.1
  663.5 5.4 slice-start.2
  673.5 1.3 copy-start.20
  676.7 87.9 %all-to-all-start = ((f32[8,4,256]{2,1,0:T(4,128)}), f32[8,4,256]{2,1,0:T(4,128)S(1)}, u32[]{:S(2)}, u32[]{:S(2)}) async-start(f32[8,4,256]{2,1,0:T(4,128)} %select_reduce_fusion.1), calls=%async_computation.1 | async-start | bytes 65536 | tf_op jit(solution)/shard_map/all_to_all | solution.py:1173
  683.7 156.7 %all-gather.4.cloned.1.call-start = ((), (), s32[]{:S(2)}) async-start(), calls=%async_computation.6 | async-start | bytes 5242880 | tf_op jit(solution)/shard_map/all_gather | solution.py:1210
  697.6 67.1 %copy-start.17 = (f32[256,32]{1,0:T(8,128)S(1)}, f32[256,32]{1,0:T(8,128)}, u32[]{:S(2)}) copy-start(f32[256,32]{1,0:T(8,128)} %get-tuple-element.142) | copy-start | bytes 98308
  697.6 67.3 %copy-start.24 = (f32[2048]{0:T(1024)S(1)}, f32[2048]{0:T(1024)}, u32[]{:S(2)}) copy-start(f32[2048]{0:T(1024)} %copy-done.23) | copy-start | bytes 24580
  697.6 67.3 %copy-start.31 = (f32[256]{0:T(256)S(1)}, f32[256]{0:T(256)}, u32[]{:S(2)}) copy-start(f32[256]{0:T(256)} %copy-done.30) | copy-start | bytes 3076
  764.6 1.6 copy-start.3
  766.2 3.1 copy-start.38
  766.2 4.5 copy-start.12
  769.3 1.3 copy-start.5
  769.3 3.0 copy-start.33
  770.6 1.8 copy-start.15
  772.4 210.9 %reduce-scatter.6.cloned.1.call-start = ((), (), s32[]{:S(2)}) async-start(), calls=%async_computation.7 | async-start | bytes 5242880 | tf_op jit(solution)/shard_map/reduce_scatter | solution.py:1232
  888.0 1.8 copy-start.22
  888.0 1.9 copy-start.21
  890.0 1.4 copy-start.18
  901.1 0.6 copy-start.35
  901.1 1.2 copy-start.8
  901.1 277.9 %reduce-scatter.8.cloned.1.call-start = ((), (), s32[]{:S(2)}) async-start(), calls=%async_computation.8 | async-start | bytes 6488064 | tf_op jit(solution)/shard_map/reduce_scatter | solution.py:1254
  903.1 0.7 copy-start.39
  903.1 1.7 copy-start.19
  916.0 67.4 %copy-start.26 = (f32[2048]{0:T(1024)S(1)}, f32[2048]{0:T(1024)}, u32[]{:S(2)}) copy-start(f32[2048]{0:T(1024)} %get-tuple-element.131) | copy-start | bytes 24580
  983.3 1.2 copy-start.11
  995.7 5.2 copy-start.6
  995.8 5.2 copy-start.40
  1000.7 99.2 %collective-permute-start.3 = (bf16[4,256,2048]{2,1,0:T(8,128)(2,1)}, bf16[4,256,2048]{2,1,0:T(8,128)(2,1)}, u32[]{:S(2)}, u32[]{:S(2)}) collective-permute-start(bf16[4,256,2048]{2,1,0:T(8,128)(2,1)} %dynamic-slice_bitcast_fusion), channel_id=1, source_target_pairs={{0,1},{1,0},{2,3},{3,2},{4,5},{5,4},{6,7},{7,6},{8,9},{9,8},{10,11... | collective-permute-start | bytes 12582920 | tf_op jit(solution)/shard_map/ppermute | solution.py:91
  1006.0 1.9 copy-start.13
  1008.2 4.4 collective-permute-start.7
  1016.8 28.2 %collective-permute-start.8 = (bf16[128,2048]{1,0:T(8,128)(2,1)}, bf16[128,2048]{1,0:T(8,128)(2,1)}, u32[]{:S(2)}, u32[]{:S(2)}) collective-permute-start(bf16[128,2048]{1,0:T(8,128)(2,1)} %get-tuple-element.155), channel_id=1, source_target_pairs={{0,2},{1,3},{2,4},{3,5},{4,6},{5,7},{6,0},{7,1},{8,10},{9,11},{10,... | collective-permute-start | bytes 1572872 | tf_op jit(solution)/shard_map/ppermute | solution.py:60
  1018.6 44.6 %collective-permute-start.10 = (bf16[128,2048]{1,0:T(8,128)(2,1)}, bf16[128,2048]{1,0:T(8,128)(2,1)}, u32[]{:S(2)}, u32[]{:S(2)}) collective-permute-start(bf16[128,2048]{1,0:T(8,128)(2,1)} %get-tuple-element.156), channel_id=1, source_target_pairs={{0,6},{1,7},{2,0},{3,1},{4,2},{5,3},{6,4},{7,5},{8,14},{9,15},{10,... | collective-permute-start | bytes 1572872 | tf_op jit(solution)/shard_map/ppermute | solution.py:60
  1020.6 76.6 %collective-permute-start.9 = (bf16[128,2048]{1,0:T(8,128)(2,1)}, bf16[128,2048]{1,0:T(8,128)(2,1)}, u32[]{:S(2)}, u32[]{:S(2)}) collective-permute-start(bf16[128,2048]{1,0:T(8,128)(2,1)} %get-tuple-element.157), channel_id=1, source_target_pairs={{0,4},{1,5},{2,6},{3,7},{4,0},{5,1},{6,2},{7,3},{8,12},{9,13},{10,... | collective-permute-start | bytes 1572872 | tf_op jit(solution)/shard_map/ppermute | solution.py:60
  1105.3 3.0 copy-start.9
  1108.3 75.1 %collective-permute-start.4 = (bf16[256,2048]{1,0:T(8,128)(2,1)}, bf16[256,2048]{1,0:T(8,128)(2,1)}, u32[]{:S(2)}, u32[]{:S(2)}) collective-permute-start(bf16[256,2048]{1,0:T(8,128)(2,1)} %get-tuple-element.147), channel_id=1, source_target_pairs={{0,2},{1,3},{2,4},{3,5},{4,6},{5,7},{6,0},{7,1},{8,10},{9,11},{10,... | collective-permute-start | bytes 3145736 | tf_op jit(solution)/shard_map/ppermute | solution.py:60
  1108.3 75.1 %collective-permute-start.6 = (bf16[256,2048]{1,0:T(8,128)(2,1)}, bf16[256,2048]{1,0:T(8,128)(2,1)}, u32[]{:S(2)}, u32[]{:S(2)}) collective-permute-start(bf16[256,2048]{1,0:T(8,128)(2,1)} %get-tuple-element.148), channel_id=1, source_target_pairs={{0,6},{1,7},{2,0},{3,1},{4,2},{5,3},{6,4},{7,5},{8,14},{9,15},{10,... | collective-permute-start | bytes 3145736 | tf_op jit(solution)/shard_map/ppermute | solution.py:60
  1112.1 88.4 %collective-permute-start.5 = (bf16[256,2048]{1,0:T(8,128)(2,1)}, bf16[256,2048]{1,0:T(8,128)(2,1)}, u32[]{:S(2)}, u32[]{:S(2)}) collective-permute-start(bf16[256,2048]{1,0:T(8,128)(2,1)} %get-tuple-element.149), channel_id=1, source_target_pairs={{0,4},{1,5},{2,6},{3,7},{4,0},{5,1},{6,2},{7,3},{8,12},{9,13},{10,... | collective-permute-start | bytes 3145736 | tf_op jit(solution)/shard_map/ppermute | solution.py:60
  1112.1 66.8 %copy-start.36 = (f32[256]{0:T(256)S(1)}, f32[256]{0:T(256)}, u32[]{:S(2)}) copy-start(f32[256]{0:T(256)} %get-tuple-element.170) | copy-start | bytes 3076
  1178.9 21.6 %copy-start.4 = (f32[256,2048]{1,0:T(8,128)S(1)}, f32[256,2048]{1,0:T(8,128)}, u32[]{:S(2)}) copy-start(f32[256,2048]{1,0:T(8,128)} %copy-done.2) | copy-start | bytes 6291460
  1178.9 21.6 %copy-start.25 = (f32[2048]{0:T(1024)S(1)}, f32[2048]{0:T(1024)}, u32[]{:S(2)}) copy-start(f32[2048]{0:T(1024)} %copy-done.23) | copy-start | bytes 24580
  1178.9 21.6 %copy-start.32 = (f32[256]{0:T(256)S(1)}, f32[256]{0:T(256)}, u32[]{:S(2)}) copy-start(f32[256]{0:T(256)} %copy-done.30) | copy-start | bytes 3076
  1178.9 21.6 %copy-start.34 = (f32[256]{0:T(256)S(1)}, f32[256]{0:T(256)}, u32[]{:S(2)}) copy-start(f32[256]{0:T(256)} %copy-done.33) | copy-start | bytes 3076
  1179.0 27.1 %all-to-all-start.1 = ((bf16[4,64,1408]{2,1,0:T(8,128)(2,1)}), bf16[4,64,1408]{2,1,0:T(8,128)(2,1)}, u32[]{:S(2)}, u32[]{:S(2)}) async-start(bf16[4,64,1408]{2,1,0:T(8,128)(2,1)} %shard_map.288), calls=%async_computation.4 | async-start | bytes 1441792 | tf_op jit(solution)/shard_map/all_to_all | solution.py:1258
  1200.5 13.0 %copy-start.1 = (bf16[64,512]{1,0:T(8,128)(2,1)S(1)}, bf16[64,512]{1,0:T(8,128)(2,1)}, u32[]{:S(2)}) copy-start(bf16[64,512]{1,0:T(8,128)(2,1)} %param.20) | copy-start | bytes 196612
Sparse Core Ops, SparseCore 0:
  106.9 273.6 all-gather.5
  663.6 91.7 reduce-scatter.3
  772.5 52.5 all-gather.3
  901.2 52.5 reduce-scatter.5
  995.8 95.8 reduce-scatter.7
where the time goes:
time: 1230 us; the launch traced here: 1220 us
  Pallas kernels  835 us (68%)
  waiting for transfers between devices  156 us (13%)
  local copies, waits for them, and re-layouts  83.1 us (7%)
  other arithmetic  58.8 us (5%)
  matrix products  48.4 us (4%)
  starting transfers between devices  24.1 us (2%)
  between operations  14.9 us (1%)
    pallas_call x4, Pallas kernels, expert_grads(): pl.pallas_call(grads_kernel, grid=(hidden // tile, parts), out_shape=[jax...  268 us
    pallas_call x1, Pallas kernels, gather_square(): pl.pallas_call(square_kernel, out_shape=jax.ShapeDtypeStruct((bands, peer...  225 us
    ppermute x6, waiting for transfers between devices, shifted(): lax.ppermute(value, axis, [(i, (i + step) % count) for i in range(count)])  92.8 us
    pallas_call x1, Pallas kernels, start_moves(): pl.pallas_call(start_kernel, out_shape=[jax.ShapeDtypeStruct(shape, BF16)...  89 us
    pallas_call x1, Pallas kernels, own_experts(): pl.pallas_call(own_kernel, grid=(owned, rows // some, hidden // tile), in...  77.2 us
    pallas_call x2, Pallas kernels, place_rows(): pl.pallas_call(place_kernel, grid_spec=pltpu.PrefetchScalarGridSpec(num_s...  67 us
    ppermute x3, waiting for transfers between devices, traded(): lax.ppermute(value, axis, [(i, i ^ step) for i in range(lax.axis_size(axi...  58.9 us
    dot_general x7, matrix products, dot(): return jnp.einsum(spec, left, right, preferred_element_type=F32)  44.5 us
  transfers between devices with their start and end apart: 18, of which 7 were waited for; matrix products, arithmetic and copies ran while one was open for 8% of the time, Pallas kernels for 45%

commit v1 on v0

--- a/solution.py
+++ b/solution.py
@@ -82,14 +82,19 @@
     return total
 
 
-def sum_peers(blocks):
+def sum_cores(blocks):
     count, me = lax.axis_size("expert"), lax.axis_index("expert")
-    core, chip, chips = lax.rem(me, 2), lax.div(me, 2), count // 2
+    core, chips = lax.rem(me, 2), count // 2
     paired = blocks.reshape(chips, 2, *blocks.shape[1:])
     sent = lax.dynamic_index_in_dim(paired, 1 - core, 1, keepdims=False)
     kept = lax.dynamic_index_in_dim(paired, core, 1, keepdims=False)
     got = lax.ppermute(sent, "expert", [(i, i ^ 1) for i in range(count)])
-    halves = (kept.astype(F32) + got.astype(F32)).astype(BF16)
+    return (kept.astype(F32) + got.astype(F32)).astype(BF16)
+
+
+def sum_chips(halves):
+    me = lax.axis_index("expert")
+    chip, chips = lax.div(me, 2), lax.axis_size("expert") // 2
     total = lax.dynamic_index_in_dim(halves, chip, 0, keepdims=False).astype(F32)
     for step in range(1, chips):
         sent = lax.dynamic_index_in_dim(halves, lax.rem(chip + step, chips), 0, keepdims=False)
@@ -1063,6 +1068,11 @@
         ],
         axis=1,
     )
+    shared = owned >= bands == 4
+    top = routes.shape[-1]
+    ride = tok_count * top // band_rows
+    if shared:
+        small = jnp.concatenate([small, routes[0].reshape(band_rows, ride).astype(BF16)], axis=1)
     small = jnp.pad(small, ((0, 0), (0, 128 - small.shape[1])))
     packed = jnp.concatenate(
         [
@@ -1082,8 +1092,6 @@
     head_gains = small_all.reshape(bands * peers, band_rows, 128)[:, :gain_rows]
     query_gain = head_gains[:, :, experts + 2].reshape(-1).astype(F32)
     key_gain = head_gains[:, :, experts + 3].reshape(-1).astype(F32)
-    shared = owned >= bands == 4
-    top = routes.shape[-1]
 
     def beside(rows, *sides):
         used = sum(side.shape[-1] for side in sides)
@@ -1095,7 +1103,7 @@
         gates = gates + sides[..., experts : 2 * experts].astype(F32)
         return lax.dynamic_slice_in_dim(gates, peer * owned, owned, axis=2)
 
-    cot_rows = beside(after(cotangent[0], out_w), routes[0])
+    cot_rows = beside(cotangent[0], routes[0])
     if shared:
         cot_all = lax.all_gather(cot_rows, ("dp", "expert"), axis=0, tiled=False)
         cot_all = cot_all.reshape(bands, peers, tok_count, -1)
@@ -1126,8 +1134,6 @@
     high = own_gates.astype(BF16)
     low = own_gates - high.astype(F32)
     moe_rows = beside(normed_moe, high, low)
-    moe_all = gather_square(moe_rows) if shared else gather_rows(moe_rows)[None]
-    cot_all = after(cot_all, moe_all)
 
     def in_order(columns):
         pick = [
@@ -1136,8 +1142,17 @@
         ]
         return jnp.concatenate(pick)
 
-    routes_all = in_order(cot_all[..., width : width + top]).astype(jnp.int32)
-    ranks_all = block_ranks(routes_all, peer, owned, experts)
+    if shared:
+        sides = small_all.reshape(bands, peers, band_rows, 128)
+        routes_all = sides[..., experts + 4 : experts + 4 + ride]
+        routes_all = in_order(routes_all.reshape(bands, peers, tok_count, top))
+        ranks_all = block_ranks(routes_all.astype(jnp.int32), peer, owned, experts)
+        moe_rows = after(moe_rows, ranks_all)
+    moe_all = gather_square(moe_rows) if shared else gather_rows(moe_rows)[None]
+    cot_all = after(cot_all, moe_all)
+    if not shared:
+        routes_all = cot_all[0, ..., width : width + top].astype(jnp.int32)
+        ranks_all = block_ranks(routes_all, peer, owned, experts)
     own_ranks = ranks_all[:peers]
     token_ranks = own_ranks.transpose(0, 2, 1)
     cot_placed = place_rows(ranks_all, cot_all, here).reshape(owned, -1, width)
@@ -1211,7 +1226,11 @@
     expert_sums, mark = next_expert(1, expert_sums, grad_branch)
     branch_all = after(branch_all, mark)
 
+    grad_output = dot("tm,td->md", attended_low, branch_all).astype(BF16)
     grad_attended = dot("td,md->tm", branch_all, out_w).astype(BF16)
+    grad_attended = after(grad_attended, grad_output)
+    grad_output = lax.psum_scatter(grad_output, "expert", scatter_dimension=0, tiled=True)
+    rows_out = sum_cores(after(rows_out, branch_all))
     query_grad, key_grad, value_grad, head_grads = attend_back(
         query_low,
         key_low,
@@ -1228,7 +1247,9 @@
     )
     qkv_grad = jnp.concatenate([query_grad, key_grad, value_grad], axis=1)
     grad_normed_attn = dot("tm,dm->td", qkv_grad, qkv_w).astype(BF16)
-    expert_sums, mark = next_expert(2, expert_sums, grad_normed_attn)
+    expert_sums, mark = next_expert(2, expert_sums, grad_normed_attn, rows_out)
+    moe_sum = sum_chips(rows_out)
+    block_out = (hidden + moe_sum).astype(BF16)
     grad_normed_attn = lax.psum_scatter(
         grad_normed_attn, "dp", scatter_dimension=0, tiled=True
     )
@@ -1262,19 +1283,13 @@
     grad_key = band_qkv[:, :, q_cols : q_cols + k_cols].astype(F32).reshape(band_rows, -1)
     grad_value = band_qkv[:, :, q_cols + k_cols : qkv_cols].astype(F32).reshape(band_rows, -1)
     smaller = jnp.sum(band_qkv[:, :, qkv_cols:].astype(F32), axis=1)
-    grad_output = sum_peers(
-        dot("tm,td->md", attended_low, branch_all).astype(BF16).reshape(peers, -1, width)
-    )
-
-    moe_sum = sum_peers(after(rows_out, branch_all))
-    block_out = (hidden + moe_sum).astype(BF16)
     return (
         block_out[None],
         grad_tokens[None],
         grad_query,
         grad_key,
         grad_value,
-        grad_output,
+        grad_output.astype(F32),
         smaller[:, :experts],
         smaller[:, experts],
         smaller[:, experts + 1],

time: 1230 us -> 1210 us (0.984)
  waiting for transfers between devices: 156 us -> 86.4 us
  Pallas kernels: 835 us -> 883 us
    pallas_call x1, Pallas kernels: 89 us -> 208 us  [start_moves(): pl.pallas_call(start_kernel, out_shape=[jax.ShapeDtypeStruct(shape, BF16)...]
    ppermute x6 -> x3, waiting for transfers between devices: 92.8 us -> 0.01 us  [shifted(): lax.ppermute(value, axis, [(i, (i + step) % count) for i in range(count)])]
    pallas_call x1, Pallas kernels: 225 us -> 155 us  [gather_square(): pl.pallas_call(square_kernel, out_shape=jax.ShapeDtypeStruct((bands, peer...]
    reduce_scatter x1, waiting for transfers between devices: 0.02 us -> 63.9 us  [on_device(): lax.psum_scatter(band_qkv.reshape(width, -1), 'expert', scatter_dimension...]
    ppermute x3, waiting for transfers between devices: 58.9 us -> 20.3 us  [traded(): lax.ppermute(value, axis, [(i, i ^ step) for i in range(lax.axis_size(axi...]
    unnamed x99 -> x104, local copies, waits for them, and re-layouts: 33.1 us -> 29.2 us
  transfers between devices with their start and end apart: 18 -> 15, of which waited for: 7 -> 3; matrix products, arithmetic and copies ran while one was open for 8% -> 11% of each run, Pallas kernels for 45% -> 60%
where the time goes in v1:
time: 1210 us; the launch traced here: 1200 us
  Pallas kernels  883 us (73%)
  waiting for transfers between devices  86.4 us (7%)
  local copies, waits for them, and re-layouts  80.5 us (7%)
  other arithmetic  58.8 us (5%)
  matrix products  51.1 us (4%)
  starting transfers between devices  19.9 us (2%)
  between operations  15.3 us (1%)
    pallas_call x4, Pallas kernels, expert_grads(): pl.pallas_call(grads_kernel, grid=(hidden // tile, parts), out_shape=[jax...  268 us
    pallas_call x1, Pallas kernels, start_moves(): pl.pallas_call(start_kernel, out_shape=[jax.ShapeDtypeStruct(shape, BF16)...  208 us
    pallas_call x1, Pallas kernels, gather_square(): pl.pallas_call(square_kernel, out_shape=jax.ShapeDtypeStruct((bands, peer...  155 us
    pallas_call x1, Pallas kernels, own_experts(): pl.pallas_call(own_kernel, grid=(owned, rows // some, hidden // tile), in...  77.1 us
    pallas_call x2, Pallas kernels, place_rows(): pl.pallas_call(place_kernel, grid_spec=pltpu.PrefetchScalarGridSpec(num_s...  67 us
    reduce_scatter x1, waiting for transfers between devices, on_device(): lax.psum_scatter(band_qkv.reshape(width, -1), 'expert', scatter_dimension...  63.9 us
    dot_general x7, matrix products, dot(): return jnp.einsum(spec, left, right, preferred_element_type=F32)  47.3 us
    pallas_call x1, Pallas kernels, attend_back(): pl.pallas_call(attend_back_kernel, grid=(heads, length // block), in_spec...  38.6 us
  transfers between devices with their start and end apart: 15, of which 3 were waited for; matrix products, arithmetic and copies ran while one was open for 11% of the time, Pallas kernels for 60%

profile of v1, /device:TPU:0, one launch (start us, length us, event | category | flops | bytes accessed | tf_op | source)
XLA Modules:
  0.0 1195.3 jit_solution(17308084425204213761)
XLA Ops:
  8.3 3.0 concatenate.62
  13.5 208.1 %shard_map.263 = (bf16[4,256,2048]{2,1,0:T(8,128)(2,1)}, bf16[4,64,1408]{2,1,0:T(8,128)(2,1)}, bf16[4,8,64,1408]{3,2,1,0:T(8,128)(2,1)}, bf16[8,128,2048]{2,1,0:T(8,128)(2,1)}) custom-call(bf16[256,2048]{1,0:T(8,128)(2,1)} %bitcast.181, bf16[4,64,1408]{2,1,0:T(8,128)(2,1)} %maximum_bitcast_fusion.pack_ref, bf16[128,2048]{1,0:T(8,128)(2,1)} %wo_ref.1), custom_call_target="tpu_custom_call" | custom-call | tf_op jit(solution)/shard_map/pallas_call | solution.py:465
  224.7 1.9 fusion.26
  226.6 1.3 pad_maximum_fusion.2
  227.9 2.6 convert_reduce_fusion
  230.6 13.1 %shard_map.264 = (bf16[1024,2048]{1,0:T(8,128)(2,1)}, f32[1024,1024]{1,0:T(8,128)}, f32[1024,128]{1,0:T(8,128)}, bf16[1024,1024]{1,0:T(8,128)(2,1)}, bf16[1024,1...) custom-call(bf16[1024,2048]{1,0:T(8,128)(2,1)} %bitcast.192, f32[1,2048]{1,0:T(1,128)} %bitcast.207, ...), custom_call_target="tpu_custom_call" | custom-call | tf_op jit(solution)/shard_map/pallas_call | solution.py:816
  243.7 1.8 copy.209
  246.5 29.6 %shard_map.265 = (bf16[1024,1024]{1,0:T(8,128)(2,1)}, f32[8,1,1024]{2,1,0:T(1,128)}) custom-call(bf16[1024,1024]{1,0:T(8,128)(2,1)} %get-tuple-element.53.q_ref, bf16[1024,128]{1,0:T(8,128)(2,1)} %get-tuple-element.54.k_ref, bf16[128,1024]{1,0:T(8,128)(2,1)} %bitcast.202, s32[1,1024]{1,0:T(1,128)} %seg_row_ref.3, s32[1024,1]{1,0:T(8,128)} %copy.210.seg_col_ref), custom_call_target="tpu_custom_call" | custom-call | tf_op jit(solution)/shard_map/pallas_call | solution.py:874
  276.2 7.3 convolution_convert_fusion.2
  283.5 1.8 dynamic-slice_bitcast_fusion.6
  286.5 3.5 collective-permute-start.2
  295.0 2.8 fusion.1
  298.1 1.9 copy.250
  300.4 2.7 copy.217
  303.0 5.0 convert_select_fusion
  308.1 3.5 copy.223.refs_1_.rank_ref
  311.5 2.9 fusion.46
  314.5 20.3 %collective-permute-done.1 = bf16[256,2048]{1,0:T(8,128)(2,1)} collective-permute-done((bf16[256,2048]{1,0:T(8,128)(2,1)}, bf16[256,2048]{1,0:T(8,128)(2,1)}, u32[]{:S(2)}, u32[]{:S(2)}) %collective-permute-start.1) | collective-permute-done | bytes 1048608 | tf_op jit(solution)/shard_map/ppermute | solution.py:64
  334.7 3.7 multiply_reduce_fusion.2
  340.1 1.9 select_reduce_fusion.2
  343.0 1.9 concatenate.61.refs_0_
  345.0 154.8 %shard_map.267.block_ref.refs_1_ = bf16[4,8,256,2176]{3,2,1,0:T(8,128)(2,1)} custom-call(bf16[256,2176]{1,0:T(8,128)(2,1)} %shard_map.266.own_ref), custom_call_target="tpu_custom_call" | custom-call | tf_op jit(solution)/shard_map/pallas_call | solution.py:383
  499.8 1.6 slice-done
  502.6 3.2 add_bitcast_fusion
  505.8 3.2 copy.226
  509.0 2.3 select_reduce_fusion
  511.4 4.1 reshape.318.g_ref.refs_0_
  515.5 33.5 %shard_map.268 = bf16[4,32,80,2048]{3,2,1,0:T(8,128)(2,1)} custom-call(s32[1]{0:T(128)} %bitcast.25._, s32[32,4,256]{2,1,0:T(4,128)} %copy.223.refs_1_.rank_ref, bf16[4,8,256,2176]{3,2,1,0:T(8,128)(2,1)} %shard_map.267.block_ref.refs_1_), custom_call_target="tpu_custom_call" | custom-call | tf_op jit(solution)/shard_map/pallas_call | solution.py:527
  549.0 33.5 %shard_map.270 = bf16[4,32,80,2048]{3,2,1,0:T(8,128)(2,1)} custom-call(s32[1]{0:T(128)} %bitcast.25._, s32[32,4,256]{2,1,0:T(4,128)} %copy.223.refs_1_.rank_ref, bf16[4,8,256,2176]{3,2,1,0:T(8,128)(2,1)} %shard_map.269.block_ref), custom_call_target="tpu_custom_call" | custom-call | tf_op jit(solution)/shard_map/pallas_call | solution.py:527
  582.5 77.1 %shard_map.271 = (bf16[4,640,768]{2,1,0:T(8,128)(2,1)}, bf16[4,640,768]{2,1,0:T(8,128)(2,1)}, bf16[4,640,768]{2,1,0:T(8,128)(2,1)}, f32[4,640,1]{2,1,0:T(8,128)}...) custom-call(bf16[4,2560,2048]{2,1,0:T(8,128)(2,1)} %bitcast.165, bf16[4,2560,2048]{2,1,0:T(8,128)(2,1)} %bitcast.170, ...), custom_call_target="tpu_custom_call" | custom-call | flops 48318382080 | bytes 79691776 | tf_op jit(solution)/shard_map/pallas_call | solution.py:643
  659.6 13.6 %shard_map.272.refs_1_ = bf16[8,256,2048]{2,1,0:T(8,128)(2,1)} custom-call(s32[8,256,4]{2,1,0:T(8,128)} %get-tuple-element.151.rank_ref.refs_0_, bf16[4,8,80,2048]{3,2,1,0:T(8,128)(2,1)} %bitcast.189), custom_call_target="tpu_custom_call" | custom-call | tf_op jit(solution)/shard_map/pallas_call | solution.py:563
  674.7 5.3 copy.277.refs_0_
  680.0 2.5 copy.286.refs_0_
  682.5 2.3 copy.291.refs_0_
  686.6 1.4 select_reduce_fusion.1
  688.0 5.9 all-to-all-start
  693.9 13.5 %shard_map.274.refs_1_.refs_0_ = bf16[8,256,2048]{2,1,0:T(8,128)(2,1)} custom-call(s32[8,256,4]{2,1,0:T(8,128)} %shard_map.273.rank_ref, bf16[4,8,80,2048]{3,2,1,0:T(8,128)(2,1)} %bitcast.188), custom_call_target="tpu_custom_call" | custom-call | tf_op jit(solution)/shard_map/pallas_call | solution.py:563
  707.5 66.9 %shard_map.276 = (f32[4,2048,768]{2,1,0:T(8,128)}, f32[4,2048,768]{2,1,0:T(8,128)}, f32[4,768,2048]{2,1,0:T(8,128)}, f32[8,128]{1,0:T(8,128)}) custom-call(bf16[4,2560,2048]{2,1,0:T(8,128)(2,1)} %bitcast.166, bf16[4,2560,2048]{2,1,0:T(8,128)(2,1)} %bitcast.171, f32[4,2560,1]{2,1,0:T(8,128)} %shard_map.275.g_ref, ...), custom_call_target="tpu_custom_call" | custom-call | flops 48318382080 | bytes 100663296 | tf_op jit(solution)/shard_map/pallas_call | solution.py:738
  776.0 3.1 multiply_reduce_fusion
  780.5 1.7 fusion.44.refs_1_
  783.2 67.0 %shard_map.279 = (f32[4,2048,768]{2,1,0:T(8,128)}, f32[4,2048,768]{2,1,0:T(8,128)}, f32[4,768,2048]{2,1,0:T(8,128)}, f32[8,128]{1,0:T(8,128)}) custom-call(bf16[4,2560,2048]{2,1,0:T(8,128)(2,1)} %bitcast.167, bf16[4,2560,2048]{2,1,0:T(8,128)(2,1)} %bitcast.172, ...), custom_call_target="tpu_custom_call", output_to_operand_aliasing={{0}: (9, {}), {1}: (10, {}), {2}: (11, {})} | custom-call | flops 48318382080 | bytes 100663296 | tf_op jit(solution)/shard_map/pallas_call | solution.py:738
  850.2 1.6 copy-done.41
  851.8 8.3 convolution_convert_fusion.1.refs_1_
  860.1 9.3 convolution_convert_fusion.4.refs_0_
  869.4 38.6 %shard_map.283 = (bf16[1024,1024]{1,0:T(8,128)(2,1)}, bf16[1024,128]{1,0:T(8,128)(2,1)}, bf16[1024,128]{1,0:T(8,128)(2,1)}, f32[8,128]{1,0:T(8,128)}) custom-call(bf16[1024,1024]{1,0:T(8,128)(2,1)} %get-tuple-element.53.q_ref, bf16[1024,128]{1,0:T(8,128)(2,1)} %get-tuple-element.54.k_ref, bf16[128,1024]{1,0:T(8,128)(2,1)} %bitcast.201, ...), custom_call_target="tpu_custom_call" | custom-call | tf_op jit(solution)/shard_map/pallas_call | solution.py:983
  908.0 1.8 constant_dynamic-update-slice_fusion.2
  910.0 1.5 copy-done.16
  911.4 9.6 fusion.4.refs_1_
  921.1 4.8 dynamic-slice_bitcast_fusion
  928.2 10.6 convolution_convert_fusion
  938.8 8.1 fusion.refs_2_
  946.9 67.1 %shard_map.285 = (f32[4,2048,768]{2,1,0:T(8,128)}, f32[4,2048,768]{2,1,0:T(8,128)}, f32[4,768,2048]{2,1,0:T(8,128)}, f32[8,128]{1,0:T(8,128)}) custom-call(bf16[4,2560,2048]{2,1,0:T(8,128)(2,1)} %bitcast.168, bf16[4,2560,2048]{2,1,0:T(8,128)(2,1)} %bitcast.173, ...), custom_call_target="tpu_custom_call", output_to_operand_aliasing={{0}: (9, {}), {1}: (10, {}), {2}: (11, {})} | custom-call | flops 48318382080 | bytes 100663296 | tf_op jit(solution)/shard_map/pallas_call | solution.py:738
  1015.2 2.3 fusion.8
  1017.9 8.6 copy_bitcast_fusion.5
  1026.6 3.7 dynamic-slice_bitcast_fusion.3
  1030.3 1.9 collective-permute-start.4
  1032.1 2.3 collective-permute-start.5
  1034.5 1.4 collective-permute-start.6
  1035.9 66.8 %shard_map.288 = (f32[4,2048,768]{2,1,0:T(8,128)}, f32[4,2048,768]{2,1,0:T(8,128)}, f32[4,768,2048]{2,1,0:T(8,128)}, f32[8,128]{1,0:T(8,128)}) custom-call(bf16[4,2560,2048]{2,1,0:T(8,128)(2,1)} %bitcast.169, bf16[4,2560,2048]{2,1,0:T(8,128)(2,1)} %bitcast.174, ...), custom_call_target="tpu_custom_call", output_to_operand_aliasing={{0}: (9, {}), {1}: (10, {}), {2}: (11, {})} | custom-call | flops 48318382080 | bytes 100663296 | tf_op jit(solution)/shard_map/pallas_call | solution.py:738
  1102.8 2.3 convert_element_type.246
  1105.0 63.9 %reduce-scatter.9.cloned.1.call-done = bf16[256,1408]{1,0:T(8,128)(2,1)} async-done(((bf16[2048,1408]{1,0:T(8,128)(2,1)}), bf16[256,1408]{1,0:T(8,128)(2,1)}) %reduce-scatter.9.cloned.1.call-update) | async-done | bytes 720912 | tf_op jit(solution)/shard_map/reduce_scatter | solution.py:1275
  1168.9 4.2 all-to-all-start.1
  1173.2 5.5 fusion.11
  1178.7 2.1 all-to-all-done.1
  (216 shorter events, 36.6 us)
Async XLA Ops:
  7.2 5.3 copy-start
  7.2 4.2 copy-start.25
  7.2 4.3 copy-start.18
  7.2 4.5 copy-start.42
  7.2 4.7 copy-start.43
  7.2 4.8 copy-start.37
  7.3 4.9 copy-start.39
  7.3 5.0 copy-start.40
  7.3 5.2 copy-start.26
  7.3 541.7 %all-gather.6.cloned.1.call-start = ((), (), s32[]{:S(2)}) async-start(), calls=%async_computation.11 | async-start | bytes 36765696 | tf_op jit(solution)/shard_map/all_gather | solution.py:1108
  11.4 763.3 %reduce-scatter.5.cloned.1.call-start = ((), (), s32[]{:S(2)}) async-start(), calls=%async_computation.6 | async-start | bytes 9437184 | tf_op jit(solution)/shard_map/reduce_scatter | solution.py:1182
  230.6 107.9 %copy-start.21 = (f32[2048]{0:T(1024)}, f32[2048]{0:T(1024)S(1)}, u32[]{:S(2)}) copy-start(f32[2048]{0:T(1024)S(1)} %get-tuple-element.130) | copy-start | bytes 24580
  230.6 14.9 %copy-start.27 = (s32[1,1024]{1,0:T(1,128)S(1)}, s32[1,1024]{1,0:T(1,128)}, u32[]{:S(2)}) copy-start(s32[1,1024]{1,0:T(1,128)} %seg_row_ref.3) | copy-start | bytes 12292
  283.5 3.0 copy-start.12
  286.5 28.0 %collective-permute-start = (bf16[256,2048]{1,0:T(8,128)(2,1)}, bf16[256,2048]{1,0:T(8,128)(2,1)}, u32[]{:S(2)}, u32[]{:S(2)}) collective-permute-start(bf16[256,2048]{1,0:T(8,128)(2,1)} %get-tuple-element.152), channel_id=1, source_target_pairs={{0,8},{8,0},{16,24},{24,16},{1,9},{9,1},{17,25},{25,17},{2,10},{10... | collective-permute-start | bytes 3145736 | tf_op jit(solution)/shard_map/ppermute | solution.py:64
  286.5 48.3 %collective-permute-start.1 = (bf16[256,2048]{1,0:T(8,128)(2,1)}, bf16[256,2048]{1,0:T(8,128)(2,1)}, u32[]{:S(2)}, u32[]{:S(2)}) collective-permute-start(bf16[256,2048]{1,0:T(8,128)(2,1)} %get-tuple-element.154), channel_id=1, source_target_pairs={{0,16},{8,24},{16,0},{24,8},{1,17},{9,25},{17,1},{25,9},{2,18},{10... | collective-permute-start | bytes 3145736 | tf_op jit(solution)/shard_map/ppermute | solution.py:64
  286.5 48.3 %collective-permute-start.2 = (bf16[256,2048]{1,0:T(8,128)(2,1)}, bf16[256,2048]{1,0:T(8,128)(2,1)}, u32[]{:S(2)}, u32[]{:S(2)}) collective-permute-start(bf16[256,2048]{1,0:T(8,128)(2,1)} %get-tuple-element.153), channel_id=1, source_target_pairs={{0,24},{8,16},{16,8},{24,0},{1,25},{9,17},{17,9},{25,1},{2,26},{10... | collective-permute-start | bytes 3145736 | tf_op jit(solution)/shard_map/ppermute | solution.py:64
  311.5 23.2 %copy-start.8 = (bf16[1,256,2048]{2,1,0:T(8,128)(2,1)S(1)}, bf16[1,256,2048]{2,1,0:T(8,128)(2,1)}, u32[]{:S(2)}) copy-start(bf16[1,256,2048]{2,1,0:T(8,128)(2,1)} %param.16) | copy-start | bytes 3145732
  338.5 1.3 copy-start.2
  338.5 1.3 copy-start.35
  338.5 1.3 copy-start.28
  340.1 4.9 copy-start.6
  499.8 1.6 slice-start
  505.8 3.2 copy-start.13
  673.1 1.2 copy-start.11
  673.1 6.8 slice-start.1
  674.7 5.3 slice-start.2
  684.8 1.3 copy-start.17
  688.0 86.4 %all-to-all-start = ((f32[8,4,256]{2,1,0:T(4,128)}), f32[8,4,256]{2,1,0:T(4,128)S(1)}, u32[]{:S(2)}, u32[]{:S(2)}) async-start(f32[8,4,256]{2,1,0:T(4,128)} %select_reduce_fusion.1), calls=%async_computation.1 | async-start | bytes 65536 | tf_op jit(solution)/shard_map/all_to_all | solution.py:1188
  693.9 156.3 %all-gather.4.cloned.1.call-start = ((), (), s32[]{:S(2)}) async-start(), calls=%async_computation.7 | async-start | bytes 5242880 | tf_op jit(solution)/shard_map/all_gather | solution.py:1225
  707.5 67.1 %copy-start.15 = (f32[256,32]{1,0:T(8,128)S(1)}, f32[256,32]{1,0:T(8,128)}, u32[]{:S(2)}) copy-start(f32[256,32]{1,0:T(8,128)} %get-tuple-element.142) | copy-start | bytes 98308
  707.5 67.2 %copy-start.22 = (f32[2048]{0:T(1024)S(1)}, f32[2048]{0:T(1024)}, u32[]{:S(2)}) copy-start(f32[2048]{0:T(1024)} %copy-done.21) | copy-start | bytes 24580
  707.5 67.3 %copy-start.29 = (f32[256]{0:T(256)S(1)}, f32[256]{0:T(256)}, u32[]{:S(2)}) copy-start(f32[256]{0:T(256)} %copy-done.28) | copy-start | bytes 3076
  774.4 1.6 copy-start.3
  776.0 3.1 copy-start.36
  776.0 4.5 copy-start.10
  779.1 1.4 copy-start.5
  779.2 1.3 copy-start.31
  780.5 1.8 copy-start.14
  782.3 231.7 %reduce-scatter.7.cloned.1.call-start = ((), (), s32[]{:S(2)}) async-start(), calls=%async_computation.8 | async-start | bytes 5242880 | tf_op jit(solution)/shard_map/reduce_scatter | solution.py:1253
  850.2 1.6 copy-start.41
  908.0 1.8 copy-start.20
  908.0 1.9 copy-start.19
  910.0 1.5 copy-start.16
  921.1 181.7 %reduce-scatter.11.cloned.1.call-start = ((), (), s32[]{:S(2)}) async-start(), calls=%async_computation.10 | async-start | bytes 4718592 | tf_op jit(solution)/shard_map/reduce_scatter | solution.py:1232
  926.0 0.7 copy-start.33
  926.0 1.2 copy-start.7
  926.0 2.0 copy-start.38
  926.0 12.8 %collective-permute-start.3 = (bf16[4,256,2048]{2,1,0:T(8,128)(2,1)}, bf16[4,256,2048]{2,1,0:T(8,128)(2,1)}, u32[]{:S(2)}, u32[]{:S(2)}) collective-permute-start(bf16[4,256,2048]{2,1,0:T(8,128)(2,1)} %dynamic-slice_bitcast_fusion), channel_id=1, source_target_pairs={{0,1},{1,0},{2,3},{3,2},{4,5},{5,4},{6,7},{7,6},{8,9},{9,8},{10,11... | collective-permute-start | bytes 12582920 | tf_op jit(solution)/shard_map/ppermute | solution.py:91
  926.4 242.5 %reduce-scatter.9.cloned.1.call-start = ((), (), s32[]{:S(2)}) async-start(), calls=%async_computation.9 | async-start | bytes 6488064 | tf_op jit(solution)/shard_map/reduce_scatter | solution.py:1275
  946.9 67.1 %copy-start.24 = (f32[2048]{0:T(1024)S(1)}, f32[2048]{0:T(1024)}, u32[]{:S(2)}) copy-start(f32[2048]{0:T(1024)} %get-tuple-element.131) | copy-start | bytes 24580
  1014.0 1.2 copy-start.9
  1030.3 142.8 %collective-permute-start.4 = (bf16[256,2048]{1,0:T(8,128)(2,1)}, bf16[256,2048]{1,0:T(8,128)(2,1)}, u32[]{:S(2)}, u32[]{:S(2)}) collective-permute-start(bf16[256,2048]{1,0:T(8,128)(2,1)} %get-tuple-element.147), channel_id=1, source_target_pairs={{0,2},{1,3},{2,4},{3,5},{4,6},{5,7},{6,0},{7,1},{8,10},{9,11},{10,... | collective-permute-start | bytes 3145736 | tf_op jit(solution)/shard_map/ppermute | solution.py:60
  1032.1 141.0 %collective-permute-start.5 = (bf16[256,2048]{1,0:T(8,128)(2,1)}, bf16[256,2048]{1,0:T(8,128)(2,1)}, u32[]{:S(2)}, u32[]{:S(2)}) collective-permute-start(bf16[256,2048]{1,0:T(8,128)(2,1)} %get-tuple-element.149), channel_id=1, source_target_pairs={{0,4},{1,5},{2,6},{3,7},{4,0},{5,1},{6,2},{7,3},{8,12},{9,13},{10,... | collective-permute-start | bytes 3145736 | tf_op jit(solution)/shard_map/ppermute | solution.py:60
  1034.5 138.7 %collective-permute-start.6 = (bf16[256,2048]{1,0:T(8,128)(2,1)}, bf16[256,2048]{1,0:T(8,128)(2,1)}, u32[]{:S(2)}, u32[]{:S(2)}) collective-permute-start(bf16[256,2048]{1,0:T(8,128)(2,1)} %get-tuple-element.148), channel_id=1, source_target_pairs={{0,6},{1,7},{2,0},{3,1},{4,2},{5,3},{6,4},{7,5},{8,14},{9,15},{10,... | collective-permute-start | bytes 3145736 | tf_op jit(solution)/shard_map/ppermute | solution.py:60
  1035.9 69.1 %copy-start.34 = (f32[256]{0:T(256)S(1)}, f32[256]{0:T(256)}, u32[]{:S(2)}) copy-start(f32[256]{0:T(256)} %get-tuple-element.167) | copy-start | bytes 3076
  1102.7 70.4 %copy-start.4 = (f32[256,2048]{1,0:T(8,128)S(1)}, f32[256,2048]{1,0:T(8,128)}, u32[]{:S(2)}) copy-start(f32[256,2048]{1,0:T(8,128)} %copy-done.2) | copy-start | bytes 6291460
  1102.7 70.4 %copy-start.23 = (f32[2048]{0:T(1024)S(1)}, f32[2048]{0:T(1024)}, u32[]{:S(2)}) copy-start(f32[2048]{0:T(1024)} %copy-done.21) | copy-start | bytes 24580
  1102.7 70.4 %copy-start.30 = (f32[256]{0:T(256)S(1)}, f32[256]{0:T(256)}, u32[]{:S(2)}) copy-start(f32[256]{0:T(256)} %copy-done.28) | copy-start | bytes 3076
  1102.7 70.4 %copy-start.32 = (f32[256]{0:T(256)S(1)}, f32[256]{0:T(256)}, u32[]{:S(2)}) copy-start(f32[256]{0:T(256)} %copy-done.31) | copy-start | bytes 3076
  1168.9 11.9 all-to-all-start.1
  1173.2 15.1 %copy-start.1 = (bf16[64,512]{1,0:T(8,128)(2,1)S(1)}, bf16[64,512]{1,0:T(8,128)(2,1)}, u32[]{:S(2)}) copy-start(bf16[64,512]{1,0:T(8,128)(2,1)} %param.20) | copy-start | bytes 196612
Sparse Core Ops, SparseCore 0:
  11.6 259.4 all-gather.5
  673.3 92.7 reduce-scatter.4
  782.4 54.2 all-gather.3
  921.2 54.2 reduce-scatter.6
  977.8 49.9 reduce-scatter.10
  1030.1 138.8 reduce-scatter.8

commit v2 on v1

--- a/solution.py
+++ b/solution.py
@@ -27,10 +27,6 @@
     return (
         values * lax.rsqrt(jnp.mean(values * values, axis=-1, keepdims=True) + EPSILON) * gain_row
     )
-
-
-def activate(gate_vals, up_vals):
-    return gate_vals * jax.nn.sigmoid(gate_vals) * up_vals
 
 
 def masked_softmax(logits, mask):
@@ -55,22 +51,8 @@
     )(value, *others)
 
 
-def shifted(value, axis, step):
-    count = lax.axis_size(axis)
-    return lax.ppermute(value, axis, [(i, (i + step) % count) for i in range(count)])
-
-
 def traded(value, axis, step):
     return lax.ppermute(value, axis, [(i, i ^ step) for i in range(lax.axis_size(axis))])
-
-
-def gather_blocks(own, axis):
-    count, me = lax.axis_size(axis), lax.axis_index(axis)
-    whole = jnp.zeros((count, *own.shape), own.dtype)
-    whole = lax.dynamic_update_index_in_dim(whole, own, me, 0)
-    for step in range(1, count):
-        whole = lax.dynamic_update_index_in_dim(whole, traded(own, axis, step), me ^ step, 0)
-    return whole
 
 
 def sum_blocks(blocks, axis):
@@ -79,26 +61,6 @@
     for step in range(1, count):
         sent = lax.dynamic_index_in_dim(blocks, me ^ step, 0, keepdims=False)
         total = total + traded(sent, axis, step).astype(F32)
-    return total
-
-
-def sum_cores(blocks):
-    count, me = lax.axis_size("expert"), lax.axis_index("expert")
-    core, chips = lax.rem(me, 2), count // 2
-    paired = blocks.reshape(chips, 2, *blocks.shape[1:])
-    sent = lax.dynamic_index_in_dim(paired, 1 - core, 1, keepdims=False)
-    kept = lax.dynamic_index_in_dim(paired, core, 1, keepdims=False)
-    got = lax.ppermute(sent, "expert", [(i, i ^ 1) for i in range(count)])
-    return (kept.astype(F32) + got.astype(F32)).astype(BF16)
-
-
-def sum_chips(halves):
-    me = lax.axis_index("expert")
-    chip, chips = lax.div(me, 2), lax.axis_size("expert") // 2
-    total = lax.dynamic_index_in_dim(halves, chip, 0, keepdims=False).astype(F32)
-    for step in range(1, chips):
-        sent = lax.dynamic_index_in_dim(halves, lax.rem(chip + step, chips), 0, keepdims=False)
-        total = total + shifted(sent, "expert", 2 * step).astype(F32)
     return total
 
 
@@ -493,11 +455,6 @@
     slots = jnp.arange(CAP, dtype=jnp.int32)
     chosen = ranks[:, :, None, :] == slots[None, None, :, None]
     return jnp.sum(jnp.where(chosen, values.transpose(0, 2, 1)[:, :, None, :], 0.0), axis=-1)
-
-
-def by_core(values, core):
-    paired = values.reshape(-1, 2, *values.shape[1:])
-    return lax.dynamic_index_in_dim(paired, core, 1, keepdims=False)
 
 
 def place_kernel(_, rank_ref, block_ref, rows_ref):
@@ -1008,7 +965,11 @@
         ],
         scratch_shapes=[pltpu.VMEM((length, head), F32), pltpu.VMEM((length, head), F32)],
         compiler_params=pltpu.CompilerParams(vmem_limit_bytes=VMEM_BYTES),
-        cost_estimate=FREE,
+        cost_estimate=pl.CostEstimate(
+            flops=14 * length * length * cols,
+            bytes_accessed=12 * length * cols,
+            transcendentals=length * length * heads,
+        ),
     )(
         query,
         key,
@@ -1103,7 +1064,7 @@
         gates = gates + sides[..., experts : 2 * experts].astype(F32)
         return lax.dynamic_slice_in_dim(gates, peer * owned, owned, axis=2)
 
-    cot_rows = beside(cotangent[0], routes[0])
+    cot_rows = beside(after(cotangent[0], out_w), routes[0])
     if shared:
         cot_all = lax.all_gather(cot_rows, ("dp", "expert"), axis=0, tiled=False)
         cot_all = cot_all.reshape(bands, peers, tok_count, -1)
@@ -1230,7 +1191,10 @@
     grad_attended = dot("td,md->tm", branch_all, out_w).astype(BF16)
     grad_attended = after(grad_attended, grad_output)
     grad_output = lax.psum_scatter(grad_output, "expert", scatter_dimension=0, tiled=True)
-    rows_out = sum_cores(after(rows_out, branch_all))
+    moe_sum = lax.psum_scatter(
+        after(rows_out, branch_all), "expert", scatter_dimension=0, tiled=True
+    )[0]
+    block_out = (hidden + moe_sum.astype(F32)).astype(BF16)
     query_grad, key_grad, value_grad, head_grads = attend_back(
         query_low,
         key_low,
@@ -1247,9 +1211,7 @@
     )
     qkv_grad = jnp.concatenate([query_grad, key_grad, value_grad], axis=1)
     grad_normed_attn = dot("tm,dm->td", qkv_grad, qkv_w).astype(BF16)
-    expert_sums, mark = next_expert(2, expert_sums, grad_normed_attn, rows_out)
-    moe_sum = sum_chips(rows_out)
-    block_out = (hidden + moe_sum).astype(BF16)
+    expert_sums, mark = next_expert(2, expert_sums, grad_normed_attn, block_out)
     grad_normed_attn = lax.psum_scatter(
         grad_normed_attn, "dp", scatter_dimension=0, tiled=True
     )

time: 1210 us -> 1120 us (0.926)
  Pallas kernels: 883 us -> 833 us
  waiting for transfers between devices: 86.4 us -> 66.5 us
    pallas_call x1, Pallas kernels: 208 us -> 89 us  [start_moves(): pl.pallas_call(start_kernel, out_shape=[jax.ShapeDtypeStruct(shape, BF16)...]
    pallas_call x1, Pallas kernels: 155 us -> 223 us  [gather_square(): pl.pallas_call(square_kernel, out_shape=jax.ShapeDtypeStruct((bands, peer...]
    reduce_scatter x1, waiting for transfers between devices: 63.9 us -> 0.02 us  [on_device(): lax.psum_scatter(band_qkv.reshape(width, -1), 'expert', scatter_dimension...]
    reduce_scatter x1, waiting for transfers between devices: 0.02 us -> 22.3 us  [on_device(): lax.psum_scatter(grad_output, 'expert', scatter_dimension=0, tiled=True)]
    ppermute x3, waiting for transfers between devices: 20.3 us -> 34.9 us  [traded(): lax.ppermute(value, axis, [(i, i ^ step) for i in range(lax.axis_size(axi...]
    unnamed x104 -> x89, local copies, waits for them, and re-layouts: 29.2 us -> 32.2 us
  transfers between devices with their start and end apart: 15 -> 12, of which waited for: 3 -> 5; matrix products, arithmetic and copies ran while one was open for 11% -> 13% of each run, Pallas kernels for 60% -> 56%
where the time goes in v2:
time: 1120 us; the launch traced here: 1110 us
  Pallas kernels  833 us (74%)
  local copies, waits for them, and re-layouts  79.5 us (7%)
  waiting for transfers between devices  66.5 us (6%)
  other arithmetic  53 us (5%)
  matrix products  52.4 us (5%)
  starting transfers between devices  15.2 us (1%)
  between operations  15.2 us (1%)
    pallas_call x4, Pallas kernels, expert_grads(): pl.pallas_call(grads_kernel, grid=(hidden // tile, parts), out_shape=[jax...  269 us
    pallas_call x1, Pallas kernels, gather_square(): pl.pallas_call(square_kernel, out_shape=jax.ShapeDtypeStruct((bands, peer...  223 us
    pallas_call x1, Pallas kernels, start_moves(): pl.pallas_call(start_kernel, out_shape=[jax.ShapeDtypeStruct(shape, BF16)...  89 us
    pallas_call x1, Pallas kernels, own_experts(): pl.pallas_call(own_kernel, grid=(owned, rows // some, hidden // tile), in...  77.1 us
    pallas_call x2, Pallas kernels, place_rows(): pl.pallas_call(place_kernel, grid_spec=pltpu.PrefetchScalarGridSpec(num_s...  67.1 us
    dot_general x7, matrix products, dot(): return jnp.einsum(spec, left, right, preferred_element_type=F32)  47.9 us
    pallas_call x1, Pallas kernels, attend_back(): pl.pallas_call(attend_back_kernel, grid=(heads, length // block), in_spec...  38.4 us
    ppermute x3, waiting for transfers between devices, traded(): lax.ppermute(value, axis, [(i, i ^ step) for i in range(lax.axis_size(axi...  34.9 us
  transfers between devices with their start and end apart: 12, of which 5 were waited for; matrix products, arithmetic and copies ran while one was open for 13% of the time, Pallas kernels for 56%

profile of v2, /device:TPU:0, one launch (start us, length us, event | category | flops | bytes accessed | tf_op | source)
XLA Modules:
  0.0 1114.8 jit_solution(6767345973679926954)
XLA Ops:
  14.0 2.3 copy.269.refs_0_
  17.4 89.0 %shard_map.263 = (bf16[4,256,2048]{2,1,0:T(8,128)(2,1)}, bf16[4,64,1408]{2,1,0:T(8,128)(2,1)}, bf16[4,8,64,1408]{3,2,1,0:T(8,128)(2,1)}, bf16[8,128,2048]{2,1,0:T(8,128)(2,1)}) custom-call(bf16[256,2048]{1,0:T(8,128)(2,1)} %bitcast.164, bf16[4,64,1408]{2,1,0:T(8,128)(2,1)} %maximum_bitcast_fusion.pack_ref, bf16[128,2048]{1,0:T(8,128)(2,1)} %wo_ref.1), custom_call_target="tpu_custom_call" | custom-call | tf_op jit(solution)/shard_map/pallas_call | solution.py:427
  106.5 3.0 concatenate.62
  112.7 1.9 fusion.21
  114.6 1.3 pad_maximum_fusion.2
  115.9 2.7 convert_reduce_fusion
  118.6 13.2 %shard_map.264 = (bf16[1024,2048]{1,0:T(8,128)(2,1)}, f32[1024,1024]{1,0:T(8,128)}, f32[1024,128]{1,0:T(8,128)}, bf16[1024,1024]{1,0:T(8,128)(2,1)}, bf16[1024,1...) custom-call(bf16[1024,2048]{1,0:T(8,128)(2,1)} %bitcast.178, f32[1,2048]{1,0:T(1,128)} %bitcast.200, ...), custom_call_target="tpu_custom_call" | custom-call | tf_op jit(solution)/shard_map/pallas_call | solution.py:773
  131.8 1.8 copy.207
  134.6 29.6 %shard_map.265 = (bf16[1024,1024]{1,0:T(8,128)(2,1)}, f32[8,1,1024]{2,1,0:T(1,128)}) custom-call(bf16[1024,1024]{1,0:T(8,128)(2,1)} %get-tuple-element.53.q_ref, bf16[1024,128]{1,0:T(8,128)(2,1)} %get-tuple-element.54.k_ref, bf16[128,1024]{1,0:T(8,128)(2,1)} %bitcast.188, s32[1,1024]{1,0:T(1,128)} %seg_row_ref.3, s32[1024,1]{1,0:T(8,128)} %copy.208.seg_col_ref), custom_call_target="tpu_custom_call" | custom-call | tf_op jit(solution)/shard_map/pallas_call | solution.py:831
  164.3 7.3 convolution_convert_fusion.2
  171.6 1.8 dynamic-slice_bitcast_fusion.2
  175.4 1.5 collective-permute-start.1
  183.2 2.8 fusion
  186.3 2.3 copy.247
  188.9 2.7 copy.215
  191.5 5.0 convert_select_fusion
  196.5 3.5 copy.221.refs_1_.rank_ref
  200.0 2.9 fusion.41
  202.9 4.9 collective-permute-done
  207.8 30.0 %collective-permute-done.2 = bf16[256,2048]{1,0:T(8,128)(2,1)} collective-permute-done((bf16[256,2048]{1,0:T(8,128)(2,1)}, bf16[256,2048]{1,0:T(8,128)(2,1)}, u32[]{:S(2)}, u32[]{:S(2)}) %collective-permute-start.2) | collective-permute-done | bytes 1048608 | tf_op jit(solution)/shard_map/ppermute | solution.py:55
  237.9 3.7 multiply_reduce_fusion.2
  241.5 1.3 copy-done.2
  243.1 1.9 select_reduce_fusion.2
  246.1 1.9 concatenate.61.refs_0_
  248.0 222.6 %shard_map.267.block_ref.refs_1_ = bf16[4,8,256,2176]{3,2,1,0:T(8,128)(2,1)} custom-call(bf16[256,2176]{1,0:T(8,128)(2,1)} %shard_map.266.own_ref), custom_call_target="tpu_custom_call" | custom-call | tf_op jit(solution)/shard_map/pallas_call | solution.py:345
  470.6 1.6 slice-done
  473.5 3.2 add_bitcast_fusion
  476.7 3.0 copy.224
  479.7 2.3 select_reduce_fusion
  482.0 4.1 reshape.311.g_ref.refs_0_
  486.1 33.5 %shard_map.268 = bf16[4,32,80,2048]{3,2,1,0:T(8,128)(2,1)} custom-call(s32[1]{0:T(128)} %bitcast.25._, s32[32,4,256]{2,1,0:T(4,128)} %copy.221.refs_1_.rank_ref, bf16[4,8,256,2176]{3,2,1,0:T(8,128)(2,1)} %shard_map.267.block_ref.refs_1_), custom_call_target="tpu_custom_call" | custom-call | tf_op jit(solution)/shard_map/pallas_call | solution.py:484
  519.6 33.6 %shard_map.271 = bf16[4,32,80,2048]{3,2,1,0:T(8,128)(2,1)} custom-call(s32[1]{0:T(128)} %bitcast.25._, s32[32,4,256]{2,1,0:T(4,128)} %copy.221.refs_1_.rank_ref, bf16[4,8,256,2176]{3,2,1,0:T(8,128)(2,1)} %shard_map.270.block_ref), custom_call_target="tpu_custom_call" | custom-call | tf_op jit(solution)/shard_map/pallas_call | solution.py:484
  553.2 77.1 %shard_map.272 = (bf16[4,640,768]{2,1,0:T(8,128)(2,1)}, bf16[4,640,768]{2,1,0:T(8,128)(2,1)}, bf16[4,640,768]{2,1,0:T(8,128)(2,1)}, f32[4,640,1]{2,1,0:T(8,128)}...) custom-call(bf16[4,2560,2048]{2,1,0:T(8,128)(2,1)} %bitcast.150, bf16[4,2560,2048]{2,1,0:T(8,128)(2,1)} %bitcast.155, ...), custom_call_target="tpu_custom_call" | custom-call | flops 48318382080 | bytes 79691776 | tf_op jit(solution)/shard_map/pallas_call | solution.py:600
  630.3 13.6 %shard_map.273.refs_1_ = bf16[8,256,2048]{2,1,0:T(8,128)(2,1)} custom-call(s32[8,256,4]{2,1,0:T(8,128)} %get-tuple-element.148.rank_ref.refs_0_, bf16[4,8,80,2048]{3,2,1,0:T(8,128)(2,1)} %bitcast.172), custom_call_target="tpu_custom_call" | custom-call | tf_op jit(solution)/shard_map/pallas_call | solution.py:520
  645.5 5.3 copy.274.refs_0_
  650.8 2.3 copy.283.refs_0_
  653.2 2.3 copy.288.refs_0_
  655.5 1.3 copy-done.15
  657.3 1.4 select_reduce_fusion.1
  658.7 7.3 all-to-all-start
  666.0 13.5 %shard_map.275.refs_1_.refs_0_ = bf16[8,256,2048]{2,1,0:T(8,128)(2,1)} custom-call(s32[8,256,4]{2,1,0:T(8,128)} %shard_map.274.rank_ref, bf16[4,8,80,2048]{3,2,1,0:T(8,128)(2,1)} %bitcast.171), custom_call_target="tpu_custom_call" | custom-call | tf_op jit(solution)/shard_map/pallas_call | solution.py:520
  679.5 67.0 %shard_map.277 = (f32[4,2048,768]{2,1,0:T(8,128)}, f32[4,2048,768]{2,1,0:T(8,128)}, f32[4,768,2048]{2,1,0:T(8,128)}, f32[8,128]{1,0:T(8,128)}) custom-call(bf16[4,2560,2048]{2,1,0:T(8,128)(2,1)} %bitcast.151, bf16[4,2560,2048]{2,1,0:T(8,128)(2,1)} %bitcast.156, f32[4,2560,1]{2,1,0:T(8,128)} %shard_map.276.g_ref, ...), custom_call_target="tpu_custom_call" | custom-call | flops 48318382080 | bytes 100663296 | tf_op jit(solution)/shard_map/pallas_call | solution.py:695
  748.1 3.1 multiply_reduce_fusion
  752.6 1.7 fusion.39.refs_1_
  754.4 67.2 %shard_map.280 = (f32[4,2048,768]{2,1,0:T(8,128)}, f32[4,2048,768]{2,1,0:T(8,128)}, f32[4,768,2048]{2,1,0:T(8,128)}, f32[8,128]{1,0:T(8,128)}) custom-call(bf16[4,2560,2048]{2,1,0:T(8,128)(2,1)} %bitcast.152, bf16[4,2560,2048]{2,1,0:T(8,128)(2,1)} %bitcast.157, ...), custom_call_target="tpu_custom_call", output_to_operand_aliasing={{0}: (9, {}), {1}: (10, {}), {2}: (11, {})} | custom-call | flops 48318382080 | bytes 100663296 | tf_op jit(solution)/shard_map/pallas_call | solution.py:695
  823.5 9.4 convolution_convert_fusion.1.refs_1_
  832.8 9.4 convolution_convert_fusion.4.refs_0_
  842.2 38.4 %shard_map.284 = (bf16[1024,1024]{1,0:T(8,128)(2,1)}, bf16[1024,128]{1,0:T(8,128)(2,1)}, bf16[1024,128]{1,0:T(8,128)(2,1)}, f32[8,128]{1,0:T(8,128)}) custom-call(bf16[1024,1024]{1,0:T(8,128)(2,1)} %get-tuple-element.53.q_ref, bf16[1024,128]{1,0:T(8,128)(2,1)} %get-tuple-element.54.k_ref, bf16[128,1024]{1,0:T(8,128)(2,1)} %bitcast.193, ...), custom_call_target="tpu_custom_call" | custom-call | flops 15032385536 | bytes 12582912 | tf_op jit(solution)/shard_map/pallas_call | solution.py:940
  880.6 1.9 constant_dynamic-update-slice_fusion.2
  882.6 1.5 copy-done.14
  884.1 9.7 fusion.3.refs_1_
  895.1 1.4 convolution_convert_fusion.3
  896.7 10.0 convolution_convert_fusion
  906.8 5.5 reduce-scatter.8.cloned.1.call-done
  912.3 2.5 fusion.13.refs_2_
  914.7 67.0 %shard_map.286 = (f32[4,2048,768]{2,1,0:T(8,128)}, f32[4,2048,768]{2,1,0:T(8,128)}, f32[4,768,2048]{2,1,0:T(8,128)}, f32[8,128]{1,0:T(8,128)}) custom-call(bf16[4,2560,2048]{2,1,0:T(8,128)(2,1)} %bitcast.153, bf16[4,2560,2048]{2,1,0:T(8,128)(2,1)} %bitcast.158, ...), custom_call_target="tpu_custom_call", output_to_operand_aliasing={{0}: (9, {}), {1}: (10, {}), {2}: (11, {})} | custom-call | flops 48318382080 | bytes 100663296 | tf_op jit(solution)/shard_map/pallas_call | solution.py:695
  983.0 2.3 fusion.7
  987.5 8.6 copy_bitcast_fusion.5
  996.2 22.3 %reduce-scatter.14.cloned.1.call-done = bf16[128,2048]{1,0:T(8,128)(2,1)} async-done(((bf16[1024,2048]{1,0:T(8,128)(2,1)}), bf16[128,2048]{1,0:T(8,128)(2,1)}) %reduce-scatter.14.cloned.1.call-update) | async-done | bytes 524304 | tf_op jit(solution)/shard_map/reduce_scatter | solution.py:1193
  1018.5 2.1 convert_element_type.218
  1020.6 67.6 %shard_map.289 = (f32[4,2048,768]{2,1,0:T(8,128)}, f32[4,2048,768]{2,1,0:T(8,128)}, f32[4,768,2048]{2,1,0:T(8,128)}, f32[8,128]{1,0:T(8,128)}) custom-call(bf16[4,2560,2048]{2,1,0:T(8,128)(2,1)} %bitcast.154, bf16[4,2560,2048]{2,1,0:T(8,128)(2,1)} %bitcast.159, ...), custom_call_target="tpu_custom_call", output_to_operand_aliasing={{0}: (9, {}), {1}: (10, {}), {2}: (11, {})} | custom-call | flops 48318382080 | bytes 100663296 | tf_op jit(solution)/shard_map/pallas_call | solution.py:695
  1088.2 4.2 all-to-all-start.1
  1092.5 4.7 fusion.10
  1097.2 3.1 all-to-all-done.1
  (195 shorter events, 42.7 us)
Async XLA Ops:
  7.2 9.1 copy-start
  7.2 9.1 copy-start.25
  7.2 512.4 %all-gather.6.cloned.1.call-start = ((), (), s32[]{:S(2)}) async-start(), calls=%async_computation.13 | async-start | bytes 36765696 | tf_op jit(solution)/shard_map/all_gather | solution.py:1069
  109.5 637.3 %reduce-scatter.6.cloned.1.call-start = ((), (), s32[]{:S(2)}) async-start(), calls=%async_computation.7 | async-start | bytes 9437184 | tf_op jit(solution)/shard_map/reduce_scatter | solution.py:1143
  118.6 122.9 %copy-start.20 = (f32[2048]{0:T(1024)}, f32[2048]{0:T(1024)S(1)}, u32[]{:S(2)}) copy-start(f32[2048]{0:T(1024)S(1)} %get-tuple-element.130) | copy-start | bytes 24580
  118.6 15.0 %copy-start.29 = (s32[1,1024]{1,0:T(1,128)S(1)}, s32[1,1024]{1,0:T(1,128)}, u32[]{:S(2)}) copy-start(s32[1,1024]{1,0:T(1,128)} %seg_row_ref.3) | copy-start | bytes 12292
  171.6 3.0 copy-start.11
  174.6 33.3 %collective-permute-start = (bf16[256,2048]{1,0:T(8,128)(2,1)}, bf16[256,2048]{1,0:T(8,128)(2,1)}, u32[]{:S(2)}, u32[]{:S(2)}) collective-permute-start(bf16[256,2048]{1,0:T(8,128)(2,1)} %get-tuple-element.149), channel_id=1, source_target_pairs={{0,8},{8,0},{16,24},{24,16},{1,9},{9,1},{17,25},{25,17},{2,10},{10... | collective-permute-start | bytes 3145736 | tf_op jit(solution)/shard_map/ppermute | solution.py:55
  175.4 32.4 %collective-permute-start.1 = (bf16[256,2048]{1,0:T(8,128)(2,1)}, bf16[256,2048]{1,0:T(8,128)(2,1)}, u32[]{:S(2)}, u32[]{:S(2)}) collective-permute-start(bf16[256,2048]{1,0:T(8,128)(2,1)} %get-tuple-element.151), channel_id=1, source_target_pairs={{0,16},{8,24},{16,0},{24,8},{1,17},{9,25},{17,1},{25,9},{2,18},{10... | collective-permute-start | bytes 3145736 | tf_op jit(solution)/shard_map/ppermute | solution.py:55
  176.9 60.9 %collective-permute-start.2 = (bf16[256,2048]{1,0:T(8,128)(2,1)}, bf16[256,2048]{1,0:T(8,128)(2,1)}, u32[]{:S(2)}, u32[]{:S(2)}) collective-permute-start(bf16[256,2048]{1,0:T(8,128)(2,1)} %get-tuple-element.150), channel_id=1, source_target_pairs={{0,24},{8,16},{16,8},{24,0},{1,25},{9,17},{17,9},{25,1},{2,26},{10... | collective-permute-start | bytes 3145736 | tf_op jit(solution)/shard_map/ppermute | solution.py:55
  180.3 5.8 copy-start.24
  200.0 37.8 %copy-start.5 = (bf16[1,256,2048]{2,1,0:T(8,128)(2,1)S(1)}, bf16[1,256,2048]{2,1,0:T(8,128)(2,1)}, u32[]{:S(2)}) copy-start(bf16[1,256,2048]{2,1,0:T(8,128)(2,1)} %param.16) | copy-start | bytes 3145732
  241.5 1.4 copy-start.2
  241.5 1.4 copy-start.33
  241.5 1.4 copy-start.26
  243.1 4.9 copy-start.7
  470.6 1.6 slice-start
  476.7 3.0 copy-start.12
  643.9 1.2 copy-start.10
  644.0 6.9 slice-start.1
  645.5 5.3 slice-start.2
  655.5 1.3 copy-start.15
  658.7 87.8 %all-to-all-start = ((f32[8,4,256]{2,1,0:T(4,128)}), f32[8,4,256]{2,1,0:T(4,128)S(1)}, u32[]{:S(2)}, u32[]{:S(2)}) async-start(f32[8,4,256]{2,1,0:T(4,128)} %select_reduce_fusion.1), calls=%async_computation.1 | async-start | bytes 65536 | tf_op jit(solution)/shard_map/all_to_all | solution.py:1149
  666.0 155.6 %all-gather.4.cloned.1.call-start = ((), (), s32[]{:S(2)}) async-start(), calls=%async_computation.8 | async-start | bytes 5242880 | tf_op jit(solution)/shard_map/all_gather | solution.py:1186
  679.5 67.1 %copy-start.13 = (f32[256,32]{1,0:T(8,128)S(1)}, f32[256,32]{1,0:T(8,128)}, u32[]{:S(2)}) copy-start(f32[256,32]{1,0:T(8,128)} %get-tuple-element.142) | copy-start | bytes 98308
  679.5 67.3 %copy-start.21 = (f32[2048]{0:T(1024)S(1)}, f32[2048]{0:T(1024)}, u32[]{:S(2)}) copy-start(f32[2048]{0:T(1024)} %copy-done.20) | copy-start | bytes 24580
  679.5 67.3 %copy-start.27 = (f32[256]{0:T(256)S(1)}, f32[256]{0:T(256)}, u32[]{:S(2)}) copy-start(f32[256]{0:T(256)} %copy-done.26) | copy-start | bytes 3076
  746.5 1.6 copy-start.3
  748.1 3.1 copy-start.34
  748.1 4.4 copy-start.9
  751.2 1.3 copy-start.4
  751.3 3.0 copy-start.30
  754.3 157.9 %reduce-scatter.8.cloned.1.call-start = ((), (), s32[]{:S(2)}) async-start(), calls=%async_computation.9 | async-start | bytes 9437184 | tf_op jit(solution)/shard_map/reduce_scatter | solution.py:1194
  821.7 1.0 copy-start.16
  821.7 160.1 %reduce-scatter.10.cloned.1.call-start = ((), (), s32[]{:S(2)}) async-start(), calls=%async_computation.10 | async-start | bytes 5242880 | tf_op jit(solution)/shard_map/reduce_scatter | solution.py:1215
  880.6 1.9 copy-start.19
  880.6 2.0 copy-start.18
  882.6 1.5 copy-start.14
  893.8 0.7 copy-start.32
  893.9 1.2 copy-start.8
  893.9 2.6 copy-start.35
  893.9 124.6 %reduce-scatter.14.cloned.1.call-start = ((), (), s32[]{:S(2)}) async-start(), calls=%async_computation.12 | async-start | bytes 4718592 | tf_op jit(solution)/shard_map/reduce_scatter | solution.py:1193
  894.5 193.8 %reduce-scatter.12.cloned.1.call-start = ((), (), s32[]{:S(2)}) async-start(), calls=%async_computation.11 | async-start | bytes 6488064 | tf_op jit(solution)/shard_map/reduce_scatter | solution.py:1237
  914.7 67.0 %copy-start.23 = (f32[2048]{0:T(1024)S(1)}, f32[2048]{0:T(1024)}, u32[]{:S(2)}) copy-start(f32[2048]{0:T(1024)} %get-tuple-element.131) | copy-start | bytes 24580
  981.7 1.2 copy-start.6
  981.7 3.5 copy-start.17
  1088.2 4.3 copy-start.22
  1088.2 4.3 copy-start.28
  1088.2 4.3 copy-start.31
  1088.2 12.0 %all-to-all-start.1 = ((bf16[4,64,1408]{2,1,0:T(8,128)(2,1)}), bf16[4,64,1408]{2,1,0:T(8,128)(2,1)}, u32[]{:S(2)}, u32[]{:S(2)}) async-start(bf16[4,64,1408]{2,1,0:T(8,128)(2,1)} %shard_map.290), calls=%async_computation.5 | async-start | bytes 1441792 | tf_op jit(solution)/shard_map/all_to_all | solution.py:1241
  1092.5 15.2 %copy-start.1 = (bf16[64,512]{1,0:T(8,128)(2,1)S(1)}, bf16[64,512]{1,0:T(8,128)(2,1)}, u32[]{:S(2)}) copy-start(bf16[64,512]{1,0:T(8,128)(2,1)} %param.20) | copy-start | bytes 196612
Sparse Core Ops, SparseCore 0:
  109.7 275.7 all-gather.5
  644.1 93.2 reduce-scatter.5
  754.5 53.5 all-gather.3
  821.8 90.4 reduce-scatter.7
  915.1 51.0 reduce-scatter.9
  968.4 49.9 reduce-scatter.13
  1020.9 62.9 reduce-scatter.11
